TPU v7x, 512 devices: a whole 4x4x16 slice. The times are simulated.
512 devices in a mesh: blk: 64 (over z_lo, y, core), aux: 8 (over z_hi, x).
Axes of the slice: x: 4, y: 4, z: 16 (z_hi: 2, z_lo: 8; z = z_hi * 8 + z_lo), core: 2. Of those that a mesh axis runs over, the one named last changes fastest.
Arguments:
- factors: bfloat16 [2048, 64, 512], P('aux', 'blk'), may hold values from -0.119628906 to 0.119628906
- occ_energy: float32 [64], P('blk'), may hold values from -1.5 to -0.3
- vir_energy: float32 [512], replicated, may hold values from 0.5 to 3
Outputs:
- pair_energy: float32 [64, 4], P('blk')
- gamma: float32 [2048, 64, 512], P('aux', 'blk')
All inputs are finite; a program needn't handle non-finite values.
Results may differ from a plain program's by a relative error of at most 0.012.
Values may be sent and summed in bfloat16 or wider, within the bound.
A program may use at most 64 MiB of HBM per device.

v0:
```python
import jax
import jax.numpy as jnp
from jax import lax
from jax.sharding import PartitionSpec as P

REACH = 3


def from_behind(x, axis, by):
    devices = lax.axis_size(axis)
    return lax.ppermute(x, axis, [(i, (i + by) % devices) for i in range(devices)])


def neighbour_above(block):
    return from_behind(block, "blk", -1)


def energies_above(values):
    return from_behind(values, "blk", -1)


def per_device(factors, occ_energy, vir_energy):
    per_block = factors.shape[1]
    blocks_reach = (REACH + per_block - 1) // per_block
    empty = jnp.zeros((factors.shape[0], factors.shape[2]), jnp.float32)
    zero_energy = jnp.zeros((), jnp.float32)
    blocks = [factors]
    eps_blocks = [occ_energy]
    moving_b = factors
    moving_e = occ_energy
    for hop in range(blocks_reach):
        moving_b = neighbour_above(moving_b)
        moving_e = energies_above(moving_e)
        blocks.append(moving_b)
        eps_blocks.append(moving_e)
    sums = [[empty] for hop in range(blocks_reach + 1)]
    energy_rows = [[zero_energy for offset in range(REACH + 1)]]
    first_b = factors[:, 0, :]
    for offset in range(REACH + 1):
        hop = offset // per_block
        second_local = offset % per_block
        second_b = blocks[hop][:, second_local, :]
        partial_value = jnp.einsum(
            "qa,qb->ab", first_b, second_b, preferred_element_type=jnp.float32
        )
        gap = (
            vir_energy[:, None]
            + vir_energy[None, :]
            - occ_energy[0]
            - eps_blocks[hop][second_local]
        )
        whole = lax.psum(partial_value.astype(jnp.bfloat16), "aux").astype(jnp.float32)
        amplitude = (-whole / gap).astype(jnp.bfloat16)
        amp_f = amplitude.astype(jnp.float32)
        energy = -jnp.sum(gap * amp_f * (2.0 * amp_f - amp_f.T))
        weight = (2.0 * amp_f - amp_f.T).astype(jnp.bfloat16)
        energy, weight = (energy, weight)
        sums[0][0] = sums[0][0] + jnp.dot(second_b, weight.T, preferred_element_type=jnp.float32)
        if offset > 0:
            sums[hop][second_local] = jnp.dot(first_b, weight, preferred_element_type=jnp.float32)
        energy_rows[0][offset] = energy
    total = jnp.stack(sums[0], axis=1)
    for hop in range(1, blocks_reach + 1):
        total = total + from_behind(
            jnp.stack(sums[hop], axis=1).astype(jnp.bfloat16), "blk", hop
        ).astype(jnp.float32)
    energy_block = jnp.stack([jnp.stack(row) for row in energy_rows])
    return (energy_block, total)


def solution(mesh):
    return jax.shard_map(
        per_device,
        mesh=mesh,
        in_specs=(P("aux", "blk", None), P("blk"), P()),
        out_specs=(P("blk", None), P("aux", "blk", None)),
        check_vma=False,
    )
```

profile of v0, /device:TPU:6, one launch (start us, length us, event | category | flops | bytes accessed | tf_op | source)
XLA Modules:
  0.0 366.7 jit_solution(11627903781994078017)
XLA Ops:
  7.2 15.2 %collective-permute-start.1 = (bf16[256,1,512]{2,0,1:T(8,128)(2,1)}, bf16[256,1,512]{2,0,1:T(8,128)(2,1)S(1)}, u32[]{:S(2)}, u32[]{:S(2)}) collective-permute-start(bf16[256,1,512]{2,0,1:T(8,128)(2,1)} %param.3), channel_id=1, source_target_pairs={{0,504},{8,0},{16,8},{24,16},{32,24},{40,32},{48,40},{56,48},{64,5... | collective-permute-start | bytes 786440 | tf_op jit(solution)/shard_map/ppermute | solution.py:11
  22.4 4.2 %collective-permute-done.1 = bf16[256,1,512]{2,0,1:T(8,128)(2,1)S(1)} collective-permute-done((bf16[256,1,512]{2,0,1:T(8,128)(2,1)}, bf16[256,1,512]{2,0,1:T(8,128)(2,1)S(1)}, u32[]{:S(2)}, u32[]{:S(2)}) %collective-permute-start.1) | collective-permute-done | bytes 262176 | tf_op jit(solution)/shard_map/ppermute | solution.py:11
  26.6 12.4 %collective-permute-start.3 = (bf16[256,1,512]{2,0,1:T(8,128)(2,1)S(1)}, bf16[256,1,512]{2,0,1:T(8,128)(2,1)S(1)}, u32[]{:S(2)}, u32[]{:S(2)}) collective-permute-start(bf16[256,1,512]{2,0,1:T(8,128)(2,1)S(1)} %collective-permute-done.1), channel_id=1, source_target_pairs={{0,504},{8,0},{16,8},{24,16},{32,24},{40,32},{48,40},{56,48},{64,5... | collective-permute-start | bytes 786440 | tf_op jit(solution)/shard_map/ppermute | solution.py:11
  39.0 2.1 convolution_convert_fusion.3
  41.2 1.7 collective-permute-done.3
  42.9 12.5 %collective-permute-start.5 = (bf16[256,1,512]{2,0,1:T(8,128)(2,1)S(1)}, bf16[256,1,512]{2,0,1:T(8,128)(2,1)S(1)}, u32[]{:S(2)}, u32[]{:S(2)}) collective-permute-start(bf16[256,1,512]{2,0,1:T(8,128)(2,1)S(1)} %collective-permute-done.3), channel_id=1, source_target_pairs={{0,504},{8,0},{16,8},{24,16},{32,24},{40,32},{48,40},{56,48},{64,5... | collective-permute-start | bytes 786440 | tf_op jit(solution)/shard_map/ppermute | solution.py:11
  57.7 1.6 collective-permute-done.5
  61.1 12.5 %collective-permute-start = (f32[1]{0:T(128)}, f32[1]{0:T(128)}, u32[]{:S(2)}, u32[]{:S(2)}) collective-permute-start(f32[1]{0:T(128)} %param.4), channel_id=1, source_target_pairs={{0,504},{8,0},{16,8},{24,16},{32,24},{40,32},{48,40},{56,48},{64,5... | collective-permute-start | bytes 20 | tf_op jit(solution)/shard_map/ppermute | solution.py:11
  75.1 12.4 %collective-permute-start.2 = (f32[1]{0:T(128)}, f32[1]{0:T(128)}, u32[]{:S(2)}, u32[]{:S(2)}) collective-permute-start(f32[1]{0:T(128)} %collective-permute-done), channel_id=1, source_target_pairs={{0,504},{8,0},{16,8},{24,16},{32,24},{40,32},{48,40},{56,48},{64,5... | collective-permute-start | bytes 20 | tf_op jit(solution)/shard_map/ppermute | solution.py:11
  88.8 12.7 %collective-permute-start.4 = (f32[1]{0:T(128)}, f32[1]{0:T(128)}, u32[]{:S(2)}, u32[]{:S(2)}) collective-permute-start(f32[1]{0:T(128)} %collective-permute-done.2), channel_id=1, source_target_pairs={{0,504},{8,0},{16,8},{24,16},{32,24},{40,32},{48,40},{56,48},{64,5... | collective-permute-start | bytes 20 | tf_op jit(solution)/shard_map/ppermute | solution.py:11
  105.5 194.6 %all-reduce.3.cloned.1.call-done = (bf16[512,512]{1,0:T(8,128)(2,1)}, bf16[512,512]{1,0:T(8,128)(2,1)}, bf16[512,512]{1,0:T(8,128)(2,1)}, bf16[512,512]{1,0:T(8,128)(2,1)}) async-done(((bf16[512,512]{1,0:T(8,128)(2,1)}, bf16[512,512]{1,0:T(8,128)(2,1)}, bf16[512,512]{1,0:T(8,128)(2,1)}, bf16[512,512]{1,0:T(8,128)(2,1)}), (bf16[512,512]{1,0:T(8,128)(2,1)}, bf16[512,512]{1,0:T(8,128)(2,1)}, ...) | async-done | bytes 2097168 | tf_op jit(solution)/shard_map/psum | solution.py:52
  300.0 3.5 broadcast_multiply_fusion
  306.4 2.5 copy.14
  312.0 4.0 %multiply_reduce_fusion.1 = (f32[]{:T(128)}, f32[]{:T(128)}, bf16[512,512]{0,1:T(8,128)(2,1)}, f32[512,512]{0,1:T(8,128)}) fusion(f32[512,512]{0,1:T(8,128)S(1)} %copy-done.6, f32[512,512]{0,1:T(8,128)S(1)} %copy.7, f32[512,512]{1,0:T(8,128)S(1)} %get-tuple-element.27, f32[]{:T(128)} %bitcast.83, f32[512]{0:T(512)S(1)} %copy-done.18, ...), kind=kLoop, calls=%fused_computation.35 | loop fusion | flops 3407870 | bytes 7866384 | tf_op jit(solution)/shard_map/reduce_sum | solution.py:55
  316.0 1.6 copy.8
  317.7 2.8 convert_bitcast_fusion
  322.4 2.2 fusion.5
  324.6 2.6 fusion.8
  331.3 2.1 collective-permute-start.8
  333.5 4.5 %collective-permute-start.7 = (bf16[256,1,512]{0,2,1:T(8,128)(2,1)S(1)}, bf16[256,1,512]{0,2,1:T(8,128)(2,1)S(1)}, u32[]{:S(2)}, u32[]{:S(2)}) collective-permute-start(bf16[256,1,512]{0,2,1:T(8,128)(2,1)S(1)} %copy-done.17), channel_id=1, source_target_pairs={{0,16},{8,24},{16,32},{24,40},{32,48},{40,56},{48,64},{56,72},{64,... | collective-permute-start | bytes 786440 | tf_op jit(solution)/shard_map/ppermute | solution.py:11
  338.0 4.2 %collective-permute-start.6 = (bf16[256,1,512]{0,2,1:T(8,128)(2,1)}, bf16[256,1,512]{0,2,1:T(8,128)(2,1)S(1)}, u32[]{:S(2)}, u32[]{:S(2)}) collective-permute-start(bf16[256,1,512]{0,2,1:T(8,128)(2,1)} %fusion.4), channel_id=1, source_target_pairs={{0,8},{8,16},{16,24},{24,32},{32,40},{40,48},{48,56},{56,64},{64,7... | collective-permute-start | bytes 786440 | tf_op jit(solution)/shard_map/ppermute | solution.py:11
  344.3 4.1 %collective-permute-done.8 = bf16[256,1,512]{0,2,1:T(8,128)(2,1)S(1)} collective-permute-done((bf16[256,1,512]{0,2,1:T(8,128)(2,1)S(1)}, bf16[256,1,512]{0,2,1:T(8,128)(2,1)S(1)}, u32[]{:S(2)}, u32[]{:S(2)}) %collective-permute-start.8) | collective-permute-done | bytes 262176 | tf_op jit(solution)/shard_map/ppermute | solution.py:11
  348.4 4.8 %collective-permute-done.7 = bf16[256,1,512]{0,2,1:T(8,128)(2,1)S(1)} collective-permute-done((bf16[256,1,512]{0,2,1:T(8,128)(2,1)S(1)}, bf16[256,1,512]{0,2,1:T(8,128)(2,1)S(1)}, u32[]{:S(2)}, u32[]{:S(2)}) %collective-permute-start.7) | collective-permute-done | bytes 262176 | tf_op jit(solution)/shard_map/ppermute | solution.py:11
  353.2 5.3 %collective-permute-done.6 = bf16[256,1,512]{0,2,1:T(8,128)(2,1)S(1)} collective-permute-done((bf16[256,1,512]{0,2,1:T(8,128)(2,1)}, bf16[256,1,512]{0,2,1:T(8,128)(2,1)S(1)}, u32[]{:S(2)}, u32[]{:S(2)}) %collective-permute-start.6) | collective-permute-done | bytes 262176 | tf_op jit(solution)/shard_map/ppermute | solution.py:11
  (62 shorter events, 22.9 us)
Async XLA Ops:
  7.2 48.3 %copy-start = (bf16[256,1,512]{2,0,1:T(8,128)(2,1)S(1)}, bf16[256,1,512]{2,0,1:T(8,128)(2,1)}, u32[]{:S(2)}) copy-start(bf16[256,1,512]{2,0,1:T(8,128)(2,1)} %param.3) | copy-start | bytes 786436
  7.2 292.9 %all-reduce.3.cloned.1.call-start = ((), (), s32[]{:S(2)}) async-start(), calls=%async_computation | async-start | bytes 4194304 | tf_op jit(solution)/shard_map/psum | solution.py:52
  7.2 19.4 %collective-permute-start.1 = (bf16[256,1,512]{2,0,1:T(8,128)(2,1)}, bf16[256,1,512]{2,0,1:T(8,128)(2,1)S(1)}, u32[]{:S(2)}, u32[]{:S(2)}) collective-permute-start(bf16[256,1,512]{2,0,1:T(8,128)(2,1)} %param.3), channel_id=1, source_target_pairs={{0,504},{8,0},{16,8},{24,16},{32,24},{40,32},{48,40},{56,48},{64,5... | collective-permute-start | bytes 786440 | tf_op jit(solution)/shard_map/ppermute | solution.py:11
  26.6 28.8 %copy-start.11 = (bf16[256,1,512]{2,0,1:T(8,128)(2,1)}, bf16[256,1,512]{2,0,1:T(8,128)(2,1)S(1)}, u32[]{:S(2)}) copy-start(bf16[256,1,512]{2,0,1:T(8,128)(2,1)S(1)} %collective-permute-done.1) | copy-start | bytes 786436
  26.6 16.3 %collective-permute-start.3 = (bf16[256,1,512]{2,0,1:T(8,128)(2,1)S(1)}, bf16[256,1,512]{2,0,1:T(8,128)(2,1)S(1)}, u32[]{:S(2)}, u32[]{:S(2)}) collective-permute-start(bf16[256,1,512]{2,0,1:T(8,128)(2,1)S(1)} %collective-permute-done.1), channel_id=1, source_target_pairs={{0,504},{8,0},{16,8},{24,16},{32,24},{40,32},{48,40},{56,48},{64,5... | collective-permute-start | bytes 786440 | tf_op jit(solution)/shard_map/ppermute | solution.py:11
  42.9 13.7 %copy-start.13 = (bf16[256,1,512]{2,0,1:T(8,128)(2,1)}, bf16[256,1,512]{2,0,1:T(8,128)(2,1)S(1)}, u32[]{:S(2)}) copy-start(bf16[256,1,512]{2,0,1:T(8,128)(2,1)S(1)} %collective-permute-done.3) | copy-start | bytes 786436
  42.9 16.4 %collective-permute-start.5 = (bf16[256,1,512]{2,0,1:T(8,128)(2,1)S(1)}, bf16[256,1,512]{2,0,1:T(8,128)(2,1)S(1)}, u32[]{:S(2)}, u32[]{:S(2)}) collective-permute-start(bf16[256,1,512]{2,0,1:T(8,128)(2,1)S(1)} %collective-permute-done.3), channel_id=1, source_target_pairs={{0,504},{8,0},{16,8},{24,16},{32,24},{40,32},{48,40},{56,48},{64,5... | collective-permute-start | bytes 786440 | tf_op jit(solution)/shard_map/ppermute | solution.py:11
  61.1 13.9 %collective-permute-start = (f32[1]{0:T(128)}, f32[1]{0:T(128)}, u32[]{:S(2)}, u32[]{:S(2)}) collective-permute-start(f32[1]{0:T(128)} %param.4), channel_id=1, source_target_pairs={{0,504},{8,0},{16,8},{24,16},{32,24},{40,32},{48,40},{56,48},{64,5... | collective-permute-start | bytes 20 | tf_op jit(solution)/shard_map/ppermute | solution.py:11
  74.3 28.6 %copy-start.18 = (f32[512]{0:T(512)S(1)}, f32[512]{0:T(512)}, u32[]{:S(2)}) copy-start(f32[512]{0:T(512)} %param.5) | copy-start | bytes 6148
  75.1 13.7 %collective-permute-start.2 = (f32[1]{0:T(128)}, f32[1]{0:T(128)}, u32[]{:S(2)}, u32[]{:S(2)}) collective-permute-start(f32[1]{0:T(128)} %collective-permute-done), channel_id=1, source_target_pairs={{0,504},{8,0},{16,8},{24,16},{32,24},{40,32},{48,40},{56,48},{64,5... | collective-permute-start | bytes 20 | tf_op jit(solution)/shard_map/ppermute | solution.py:11
  88.8 14.2 %collective-permute-start.4 = (f32[1]{0:T(128)}, f32[1]{0:T(128)}, u32[]{:S(2)}, u32[]{:S(2)}) collective-permute-start(f32[1]{0:T(128)} %collective-permute-done.2), channel_id=1, source_target_pairs={{0,504},{8,0},{16,8},{24,16},{32,24},{40,32},{48,40},{56,48},{64,5... | collective-permute-start | bytes 20 | tf_op jit(solution)/shard_map/ppermute | solution.py:11
  310.3 1.7 copy-start.7
  316.0 1.7 copy-start.16
  322.4 2.2 copy-start.1
  322.4 2.2 copy-start.3
  327.2 3.8 %copy-start.5 = (bf16[512,512]{0,1:T(8,128)(2,1)S(1)}, bf16[512,512]{0,1:T(8,128)(2,1)}, u32[]{:S(2)}) copy-start(bf16[512,512]{0,1:T(8,128)(2,1)} %get-tuple-element.20) | copy-start | bytes 1572868
  327.2 6.3 %copy-start.17 = (bf16[256,1,512]{0,2,1:T(8,128)(2,1)S(1)}, bf16[256,1,512]{0,2,1:T(8,128)(2,1)}, u32[]{:S(2)}) copy-start(bf16[256,1,512]{0,2,1:T(8,128)(2,1)} %fusion.5) | copy-start | bytes 786436
  327.2 15.6 %copy-start.12 = (bf16[256,1,512]{2,0,1:T(8,128)(2,1)S(1)}, bf16[256,1,512]{2,0,1:T(8,128)(2,1)}, u32[]{:S(2)}) copy-start(bf16[256,1,512]{2,0,1:T(8,128)(2,1)} %copy-done.11) | copy-start | bytes 786436
  331.0 11.8 %copy-start.4 = (bf16[512,512]{1,0:T(8,128)(2,1)S(1)}, bf16[512,512]{1,0:T(8,128)(2,1)}, u32[]{:S(2)}) copy-start(bf16[512,512]{1,0:T(8,128)(2,1)} %get-tuple-element.22) | copy-start | bytes 1572868
  331.0 11.8 %copy-start.8 = (f32[512,256]{1,0:T(8,128)S(1)}, f32[512,256]{1,0:T(8,128)}, u32[]{:S(2)}) copy-start(f32[512,256]{1,0:T(8,128)} %fusion.19) | copy-start | bytes 1572868
  331.3 17.1 %collective-permute-start.8 = (bf16[256,1,512]{0,2,1:T(8,128)(2,1)S(1)}, bf16[256,1,512]{0,2,1:T(8,128)(2,1)S(1)}, u32[]{:S(2)}, u32[]{:S(2)}) collective-permute-start(bf16[256,1,512]{0,2,1:T(8,128)(2,1)S(1)} %fusion.6), channel_id=1, source_target_pairs={{0,24},{8,32},{16,40},{24,48},{32,56},{40,64},{48,72},{56,80},{64,... | collective-permute-start | bytes 786440 | tf_op jit(solution)/shard_map/ppermute | solution.py:11
  333.5 19.7 %collective-permute-start.7 = (bf16[256,1,512]{0,2,1:T(8,128)(2,1)S(1)}, bf16[256,1,512]{0,2,1:T(8,128)(2,1)S(1)}, u32[]{:S(2)}, u32[]{:S(2)}) collective-permute-start(bf16[256,1,512]{0,2,1:T(8,128)(2,1)S(1)} %copy-done.17), channel_id=1, source_target_pairs={{0,16},{8,24},{16,32},{24,40},{32,48},{40,56},{48,64},{56,72},{64,... | collective-permute-start | bytes 786440 | tf_op jit(solution)/shard_map/ppermute | solution.py:11
  338.0 20.4 %collective-permute-start.6 = (bf16[256,1,512]{0,2,1:T(8,128)(2,1)}, bf16[256,1,512]{0,2,1:T(8,128)(2,1)S(1)}, u32[]{:S(2)}, u32[]{:S(2)}) collective-permute-start(bf16[256,1,512]{0,2,1:T(8,128)(2,1)} %fusion.4), channel_id=1, source_target_pairs={{0,8},{8,16},{16,24},{24,32},{32,40},{40,48},{48,56},{56,64},{64,7... | collective-permute-start | bytes 786440 | tf_op jit(solution)/shard_map/ppermute | solution.py:11
  343.9 14.5 %copy-start.10 = (bf16[256,1,512]{2,0,1:T(8,128)(2,1)S(1)}, bf16[256,1,512]{2,0,1:T(8,128)(2,1)}, u32[]{:S(2)}) copy-start(bf16[256,1,512]{2,0,1:T(8,128)(2,1)} %copy-done.9) | copy-start | bytes 786436
  (5 other events, 5.7 us)
Sparse Core Ops, SparseCore 0:
  61.3 238.7 all-reduce.2
where the time goes:
time: 367 us
  waiting for transfers between devices  220 us (60%)
  starting transfers between devices  88.6 us (24%)
  between operations  17.6 us (5%)
  local copies, waits for them, and re-layouts  14.9 us (4%)
  other arithmetic  14.3 us (4%)
  matrix products  11.5 us (3%)
    psum x1, waiting for transfers between devices, per_device(): lax.psum(partial_value.astype(jnp.bfloat16), 'aux').astype(jnp.float32)  195 us
    ppermute x9, starting transfers between devices, from_behind(): lax.ppermute(x, axis, [(i, (i + by) % devices) for i in range(devices)])  88.5 us
    ppermute x9, waiting for transfers between devices, from_behind(): lax.ppermute(x, axis, [(i, (i + by) % devices) for i in range(devices)])  25.2 us
  transfers between devices with their start and end apart: 10, of which 10 were waited for; matrix products, arithmetic and copies ran while one was open for 2% of the time, Pallas kernels for 0%

commit v1 on v0

v1 whole, which is shorter than its diff:
```python
import jax
import jax.numpy as jnp
from jax import lax
from jax.experimental import pallas as pl
from jax.experimental.pallas import tpu as pltpu
from jax.sharding import PartitionSpec as P

MESH = pl.DeviceIdType.MESH
BF = jnp.bfloat16
F32 = jnp.float32
NX = 4
NU = 64
HALF = NU // 2
COPIES = 72


def place(x, u, k):
    u = lax.rem(u, NU)
    return lax.rem(u, HALF) * 2 + k, lax.div(u, HALF) * NX + lax.rem(x, NX)


def nt(lhs, rhs):
    return lax.dot_general(lhs, rhs, (((1,), (1,)), ((), ())), preferred_element_type=F32)


def kernel(
    f_ref, occ_ref, vir_ref, gamma_ref, energy_ref,
    bo, bx, sf, sg, rf, rg, t, a0, vv, acc, acc2, w, wt,
    gown, goth, gf, out3, in3, eps, esum, en, send, recv,
):
    b = lax.axis_index("blk")
    a = lax.axis_index("aux")
    k = lax.rem(b, 2)
    h = lax.div(a, NX)
    x = lax.rem(a, NX)
    u = HALF * h + lax.div(b, 2)
    g = NX * h + x
    near = NX * h
    far = NX * (1 - h)
    gfar = far + x
    xs = [place(x + d, u, k) for d in (1, 2, 3)]
    partner = place(x, u + HALF, k)
    twin = place(x, u, 1 - k)
    down1, down2 = place(x, u + NU - 1, k), place(x, u + NU - 2, k)
    up1, up2 = place(x, u + 1, k), place(x, u + 2, k)
    h_down1 = lax.div(lax.rem(u + NU - 1, NU), HALF)
    h_down2 = lax.div(lax.rem(u + NU - 2, NU), HALF)
    g_up1 = NX * lax.div(lax.rem(u + 1, NU), HALF) + x
    g_up2 = (1 - k) * (NX * lax.div(lax.rem(u + 2, NU), HALF) + x) + k * g
    mine = pl.ds(pl.multiple_of(32 * x, 32), 32)

    barrier = pltpu.get_barrier_semaphore()
    others = xs + [partner, twin, down1, down2, up1, up2]
    for device in others:
        pl.semaphore_signal(barrier, inc=1, device_id=device, device_id_type=MESH)

    used = []

    def copy(src, dst, device):
        n = len(used)
        made = pltpu.make_async_remote_copy(
            src_ref=src, dst_ref=dst, send_sem=send.at[n], recv_sem=recv.at[n],
            device_id=device, device_id_type=MESH,
        )
        used.append(made)
        return made

    def even(body):
        pl.when(k == 0)(body)

    def odd(body):
        pl.when(k == 1)(body)

    bo[g] = f_ref[...].T.reshape(4, 128, 256)
    eps[0] = jnp.full((8, 512), occ_ref[0], F32)
    row = jnp.broadcast_to(vir_ref[...], (128, 512))
    for q in range(4):
        column = jnp.broadcast_to(row[:, 128 * q:128 * q + 128].T[:, 0:1], (128, 512))
        vv[q] = column + row
    esum[...] = jnp.zeros_like(esum)

    pl.semaphore_wait(barrier, len(others))

    cz = [copy(bo.at[g, q], bo.at[g, q], partner) for q in range(4)]
    cx = [copy(bo.at[g], bo.at[g], xs[d]) for d in range(3)]
    ce = [copy(eps.at[0], eps.at[n], device) for n, device in ((1, twin), (2, down1), (3, down2))]
    for c in cz + cx + ce:
        c.start()
    near4, far4 = pl.ds(near, NX), pl.ds(far, NX)
    ct_near = copy(bo.at[near4], bx.at[near4], twin)
    cf_near = copy(bo.at[near4, :, mine], sf.at[near4], down1)
    cg_near = copy(bo.at[near4, :, mine], sg.at[near4], down2)
    for c in cx:
        c.wait_recv()
    ct_near.start()
    cf_near.start()
    even(cg_near.start)

    def gram(dst, lhs, rhs, base, init):
        @pl.loop(0, 2)
        def _(c):
            total = None
            for n in range(NX):
                part = nt(lhs[base + n].reshape(512, 256), rhs[base + n, pl.ds(2 * c, 2)].reshape(256, 256))
                total = part if total is None else total + part
            cols = pl.ds(pl.multiple_of(256 * c, 256), 256)
            dst[:, cols] = total if init else dst[:, cols] + total

    gram(acc, bo, bo, near, True)
    ct_near.wait_recv()
    odd(lambda: gram(acc2, bo, bx, near, True))

    cxf = [[copy(bo.at[gfar, q], bo.at[gfar, q], xs[d]) for d in range(3)] for q in range(4)]
    ct_far = [copy(bo.at[far4, q], bx.at[far4, q], twin) for q in range(4)]
    cf_far = [copy(bo.at[far4, q, mine], sf.at[far4, q], down1) for q in range(4)]
    cg_far = [copy(bo.at[far4, q, mine], sg.at[far4, q], down2) for q in range(4)]
    for q in range(5):
        if q < 4:
            cz[q].wait_recv()
            for c in cxf[q]:
                c.start()
        if q > 0:
            for c in cxf[q - 1]:
                c.wait_recv()
            cf_far[q - 1].start()
            even(cg_far[q - 1].start)
            ct_far[q - 1].start()
    cr_f = copy(bo.at[NX * h_down1 + x], rf, down1)
    cr_g = copy(bo.at[NX * h_down2 + x], rg, down2)
    cr_f.start()
    even(cr_g.start)

    for c in ce[:2]:
        c.wait_recv()
    ce[2].wait_recv()
    for c in [cf_near] + cf_far + ct_far:
        c.wait_recv()

    def amplitude(integral, first, second, q, rows):
        gap = vv[q, rows] - eps[first, 0:1, :] - eps[second, 0:1, :]
        return (-integral / gap).astype(BF)

    def sliced(p, piece, whole, first, second):
        halves = []
        for half in range(2):
            total = None
            for n in range(NX):
                group = NX * half + n
                part = nt(piece[group].reshape(128, 256), whole[group].reshape(512, 256))
                total = part if total is None else total + part
            halves.append(total)
        total = halves[0] + halves[1]
        for q in range(4):
            t[p, q, mine] = amplitude(total[32 * q:32 * q + 32], first, second, q, mine)

    ca = [[copy(t.at[p, :, mine], t.at[p, :, mine], xs[d]) for d in range(3)] for p in range(3)]
    sliced(0, sf, bo, 0, 2)
    for c in ca[0]:
        c.start()
    sliced(1, sf, bx, 1, 2)
    for c in ca[1]:
        c.start()

    @even
    def _():
        for c in [cg_near] + cg_far:
            c.wait_recv()
        sliced(2, sg, bx, 1, 3)
        for c in ca[2]:
            c.start()

    def pair(read, first, second, slot, both):
        @pl.loop(0, 4)
        def _(q):
            rows = pl.ds(pl.multiple_of(128 * q, 128), 128)
            tq = read(q, slice(None)).astype(F32)
            turned = jnp.concatenate([read(n, rows).T for n in range(4)], axis=1).astype(F32)
            wide = 2.0 * tq - turned
            gap = vv[q] - eps[first, 0:1, :] - eps[second, 0:1, :]
            esum[slot, 0:1] += jnp.sum(gap * tq * wide, axis=0, keepdims=True)
            if both:
                wt[rows] = wide.astype(BF)
            w[rows] = (2.0 * turned - tq).astype(BF)

    def times(weight, factor):
        return jnp.dot(weight[...], factor, preferred_element_type=F32)

    gram(acc, bo, bo, far, False)

    @pl.loop(0, 4)
    def _(q):
        rows = pl.ds(pl.multiple_of(128 * q, 128), 128)
        a0[q] = amplitude(acc[rows], 0, 0, q, slice(None))

    pair(lambda q, cols: a0[q, :, cols], 0, 0, 0, False)
    gown[...] = times(w, bo[g].reshape(512, 256))

    @odd
    def _():
        gram(acc2, bo, bx, far, False)

        @pl.loop(0, 4)
        def _(q):
            rows = pl.ds(pl.multiple_of(128 * q, 128), 128)
            t[2, q] = amplitude(acc2[rows], 1, 0, q, slice(None))
        rg[...] = bo[g]

    c_f = copy(out3.at[0], in3.at[0], up1)
    c_g = copy(out3.at[1], in3.at[1], up2)
    c_x = copy(out3.at[2], in3.at[2], twin)
    c_e = copy(en.at[0], en.at[1], twin)

    cr_f.wait_recv()
    for c in ca[0]:
        c.wait_recv()
    pair(lambda q, cols: t[0, q, :, cols], 0, 2, 2, True)
    gown[...] += times(w, rf[...].reshape(512, 256))
    gf[...] = times(wt, bo[g_up1].reshape(512, 256))
    for c in ca[1]:
        c.wait_recv()
    pair(lambda q, cols: t[1, q, :, cols], 1, 2, 1, True)
    out3[0] = (gf[...] + times(wt, bx[g_up1].reshape(512, 256))).astype(BF)
    c_f.start()
    goth[...] = times(w, rf[...].reshape(512, 256))

    @even
    def _():
        for c in ca[2]:
            c.wait_recv()
        cr_g.wait_recv()
        pair(lambda q, cols: t[2, q, :, cols], 1, 3, 3, True)

    @odd
    def _():
        pair(lambda q, cols: t[2, q, :, cols], 1, 0, 3, True)

    gf[...] = times(wt, bx[g_up2].reshape(512, 256))

    @even
    def _():
        out3[1] = gf[...].astype(BF)
        c_g.start()

    out3[2] = (goth[...] + times(w, rg[...].reshape(512, 256))).astype(BF)
    c_x.start()

    lane = lax.broadcasted_iota(jnp.int32, (8, 128), 1)
    total = [-jnp.sum(esum[n, 0:1], axis=1, keepdims=True) for n in range(4)]
    first_at = 1 + 2 * k
    en[0] = jnp.where(lane == first_at, total[1], jnp.where(lane == 4 - first_at, total[3], 0.0))
    c_e.start()
    kept = jnp.where(lane == 0, total[0], jnp.where(lane == 2, total[2], 0.0))
    c_e.wait_recv()
    energy_ref[...] = (kept + en[1])[0:1, 0:4]

    @odd
    def _():
        gown[...] += gf[...]

    c_x.wait_recv()
    gown[...] += in3[2].astype(F32)
    c_f.wait_recv()
    gown[...] += in3[0].astype(F32)

    @even
    def _():
        c_g.wait_recv()
        gown[...] += in3[1].astype(F32)

    for n in range(4):
        gamma_ref[:, 128 * n:128 * n + 128] = gown[128 * n:128 * n + 128].T

    only_even = [cg_near, cr_g, c_g] + cg_far + ca[2]
    for c in used:
        if all(c is not e for e in only_even):
            c.wait_send()

    @even
    def _():
        for c in only_even:
            c.wait_send()


def per_device(factors, occ_energy, vir_energy):
    vmem = pl.BlockSpec(memory_space=pltpu.VMEM)
    gamma, energy = pl.pallas_call(
        kernel,
        out_shape=(
            jax.ShapeDtypeStruct((256, 512), F32),
            jax.ShapeDtypeStruct((1, 4), F32),
        ),
        in_specs=[vmem, pl.BlockSpec(memory_space=pltpu.SMEM), vmem],
        out_specs=(vmem, vmem),
        scratch_shapes=[
            pltpu.VMEM((8, 4, 128, 256), BF),
            pltpu.VMEM((8, 4, 128, 256), BF),
            pltpu.VMEM((8, 4, 32, 256), BF),
            pltpu.VMEM((8, 4, 32, 256), BF),
            pltpu.VMEM((4, 128, 256), BF),
            pltpu.VMEM((4, 128, 256), BF),
            pltpu.VMEM((3, 4, 128, 512), BF),
            pltpu.VMEM((4, 128, 512), BF),
            pltpu.VMEM((4, 128, 512), F32),
            pltpu.VMEM((512, 512), F32),
            pltpu.VMEM((512, 512), F32),
            pltpu.VMEM((512, 512), BF),
            pltpu.VMEM((512, 512), BF),
            pltpu.VMEM((512, 256), F32),
            pltpu.VMEM((512, 256), F32),
            pltpu.VMEM((512, 256), F32),
            pltpu.VMEM((3, 512, 256), BF),
            pltpu.VMEM((3, 512, 256), BF),
            pltpu.VMEM((4, 8, 512), F32),
            pltpu.VMEM((4, 8, 512), F32),
            pltpu.VMEM((2, 8, 128), F32),
            pltpu.SemaphoreType.DMA((COPIES,)),
            pltpu.SemaphoreType.DMA((COPIES,)),
        ],
        compiler_params=pltpu.CompilerParams(
            collective_id=0, has_side_effects=True, vmem_limit_bytes=44 << 20
        ),
        name="pairs",
    )(factors.reshape(256, 512), occ_energy, vir_energy.reshape(1, 512))
    return energy, gamma.reshape(256, 1, 512)


def solution(mesh):
    return jax.shard_map(
        per_device,
        mesh=mesh,
        in_specs=(P("aux", "blk", None), P("blk"), P()),
        out_specs=(P("blk", None), P("aux", "blk", None)),
        check_vma=False,
    )
```

time: 367 us -> 93 us (0.25)
  the two profiles are of different devices: /device:TPU:6 before, /device:TPU:8 now
where the time goes in v1:
time: 93 us; the launch traced here: 92.9 us
  Pallas kernels  88.1 us (95%)
  local copies, waits for them, and re-layouts  3.47 us (4%)
  between operations  1.29 us (1%)
    pallas_call x1, Pallas kernels, per_device(): pl.pallas_call(kernel, out_shape=(jax.ShapeDtypeStruct((256, 512), F32),...  88.1 us
    unnamed x6, local copies, waits for them, and re-layouts  3.47 us

profile of v1, /device:TPU:8, one launch (start us, length us, event | category | flops | bytes accessed | tf_op | source)
XLA Modules:
  0.0 92.9 jit_solution(5018731881970929669)
XLA Ops:
  1.3 0.0 copy-start.1
  1.3 0.7 copy-done.1
  2.0 0.0 copy-start
  2.0 0.9 %copy-done = bf16[256,1,512]{2,0,1:T(8,128)(2,1)S(1)} copy-done((bf16[256,1,512]{2,0,1:T(8,128)(2,1)S(1)}, bf16[256,1,512]{2,0,1:T(8,128)(2,1)}, u32[]{:S(2)}) %copy-start) | copy-done | bytes 262168
  2.9 88.1 %pairs.1 = (f32[256,512]{1,0:T(8,128)S(1)}, f32[1,4]{1,0:T(1,128)S(1)}) custom-call(bf16[256,512]{1,0:T(8,128)(2,1)S(1)} %bitcast.4, f32[1]{0:T(128)S(6)} %copy.7.occ_ref, f32[1,512]{1,0:T(1,128)S(1)} %bitcast.5), custom_call_target="tpu_custom_call" | custom-call | tf_op jit(solution)/shard_map/pairs/pallas_call | solution.py:286
  91.0 1.3 %copy.5 = f32[256,1,512]{2,1,0:T(1,128)} copy(f32[256,1,512]{2,0,1:T(8,128)S(1)} %bitcast.3) | data formatting | bytes 1048576
  92.4 0.5 copy.8
Async XLA Ops:
  1.3 0.7 copy-start.1
  2.0 0.9 %copy-start = (bf16[256,1,512]{2,0,1:T(8,128)(2,1)S(1)}, bf16[256,1,512]{2,0,1:T(8,128)(2,1)}, u32[]{:S(2)}) copy-start(bf16[256,1,512]{2,0,1:T(8,128)(2,1)} %param.3) | copy-start | bytes 786436

commit v2 on v1

--- a/solution.py
+++ b/solution.py
@@ -34,6 +34,7 @@
     h = lax.div(a, NX)
     x = lax.rem(a, NX)
     u = HALF * h + lax.div(b, 2)
+    y = lax.rem(u, 4)
     g = NX * h + x
     near = NX * h
     far = NX * (1 - h)
@@ -54,16 +55,21 @@
     for device in others:
         pl.semaphore_signal(barrier, inc=1, device_id=device, device_id_type=MESH)
 
-    used = []
-
-    def copy(src, dst, device):
+    used, done = [], []
+
+    def copy(src, dst, device, only_even=False):
         n = len(used)
         made = pltpu.make_async_remote_copy(
             src_ref=src, dst_ref=dst, send_sem=send.at[n], recv_sem=recv.at[n],
             device_id=device, device_id_type=MESH,
         )
-        used.append(made)
+        used.append((made, only_even))
         return made
+
+    def sent(*copies):
+        for c in copies:
+            c.wait_send()
+            done.append(c)
 
     def even(body):
         pl.when(k == 0)(body)
@@ -84,17 +90,25 @@
     cz = [copy(bo.at[g, q], bo.at[g, q], partner) for q in range(4)]
     cx = [copy(bo.at[g], bo.at[g], xs[d]) for d in range(3)]
     ce = [copy(eps.at[0], eps.at[n], device) for n, device in ((1, twin), (2, down1), (3, down2))]
-    for c in cz + cx + ce:
+    cr_f = copy(bo.at[NX * h_down1 + x], rf, down1)
+    cr_g = copy(bo.at[NX * h_down2 + x], rg, down2, True)
+    for c in cz[:2] + cx + ce:
         c.start()
+    pl.when(y > 0)(cr_f.start)
+    pl.when((y > 1) & (k == 0))(cr_g.start)
     near4, far4 = pl.ds(near, NX), pl.ds(far, NX)
     ct_near = copy(bo.at[near4], bx.at[near4], twin)
     cf_near = copy(bo.at[near4, :, mine], sf.at[near4], down1)
-    cg_near = copy(bo.at[near4, :, mine], sg.at[near4], down2)
+    cg_near = copy(bo.at[near4, :, mine], sg.at[near4], down2, True)
+    sent(cz[0])
+    cz[2].start()
     for c in cx:
         c.wait_recv()
     ct_near.start()
     cf_near.start()
     even(cg_near.start)
+    sent(cz[1])
+    cz[3].start()
 
     def gram(dst, lhs, rhs, base, init):
         @pl.loop(0, 2)
@@ -113,7 +127,7 @@
     cxf = [[copy(bo.at[gfar, q], bo.at[gfar, q], xs[d]) for d in range(3)] for q in range(4)]
     ct_far = [copy(bo.at[far4, q], bx.at[far4, q], twin) for q in range(4)]
     cf_far = [copy(bo.at[far4, q, mine], sf.at[far4, q], down1) for q in range(4)]
-    cg_far = [copy(bo.at[far4, q, mine], sg.at[far4, q], down2) for q in range(4)]
+    cg_far = [copy(bo.at[far4, q, mine], sg.at[far4, q], down2, True) for q in range(4)]
     for q in range(5):
         if q < 4:
             cz[q].wait_recv()
@@ -125,10 +139,8 @@
             cf_far[q - 1].start()
             even(cg_far[q - 1].start)
             ct_far[q - 1].start()
-    cr_f = copy(bo.at[NX * h_down1 + x], rf, down1)
-    cr_g = copy(bo.at[NX * h_down2 + x], rg, down2)
-    cr_f.start()
-    even(cr_g.start)
+    pl.when(y == 0)(cr_f.start)
+    pl.when((y < 2) & (k == 0))(cr_g.start)
 
     for c in ce[:2]:
         c.wait_recv()
@@ -153,13 +165,7 @@
         for q in range(4):
             t[p, q, mine] = amplitude(total[32 * q:32 * q + 32], first, second, q, mine)
 
-    ca = [[copy(t.at[p, :, mine], t.at[p, :, mine], xs[d]) for d in range(3)] for p in range(3)]
-    sliced(0, sf, bo, 0, 2)
-    for c in ca[0]:
-        c.start()
-    sliced(1, sf, bx, 1, 2)
-    for c in ca[1]:
-        c.start()
+    ca = [[copy(t.at[p, :, mine], t.at[p, :, mine], xs[d], p == 2) for d in range(3)] for p in range(3)]
 
     @even
     def _():
@@ -168,6 +174,15 @@
         sliced(2, sg, bx, 1, 3)
         for c in ca[2]:
             c.start()
+
+    sliced(0, sf, bo, 0, 2)
+
+    @odd
+    def _():
+        for c in ca[0]:
+            c.start()
+
+    sliced(1, sf, bx, 1, 2)
 
     def pair(read, first, second, slot, both):
         @pl.loop(0, 4)
@@ -192,8 +207,18 @@
         rows = pl.ds(pl.multiple_of(128 * q, 128), 128)
         a0[q] = amplitude(acc[rows], 0, 0, q, slice(None))
 
+    @even
+    def _():
+        for c in ca[2]:
+            c.wait_send()
+        for c in ca[0]:
+            c.start()
+    done.extend(ca[2])
+
     pair(lambda q, cols: a0[q, :, cols], 0, 0, 0, False)
     gown[...] = times(w, bo[g].reshape(512, 256))
+
+    c_g = copy(out3.at[1], in3.at[1], up1, True)
 
     @odd
     def _():
@@ -204,24 +229,7 @@
             rows = pl.ds(pl.multiple_of(128 * q, 128), 128)
             t[2, q] = amplitude(acc2[rows], 1, 0, q, slice(None))
         rg[...] = bo[g]
-
-    c_f = copy(out3.at[0], in3.at[0], up1)
-    c_g = copy(out3.at[1], in3.at[1], up2)
-    c_x = copy(out3.at[2], in3.at[2], twin)
-    c_e = copy(en.at[0], en.at[1], twin)
-
-    cr_f.wait_recv()
-    for c in ca[0]:
-        c.wait_recv()
-    pair(lambda q, cols: t[0, q, :, cols], 0, 2, 2, True)
-    gown[...] += times(w, rf[...].reshape(512, 256))
-    gf[...] = times(wt, bo[g_up1].reshape(512, 256))
-    for c in ca[1]:
-        c.wait_recv()
-    pair(lambda q, cols: t[1, q, :, cols], 1, 2, 1, True)
-    out3[0] = (gf[...] + times(wt, bx[g_up1].reshape(512, 256))).astype(BF)
-    c_f.start()
-    goth[...] = times(w, rf[...].reshape(512, 256))
+        pair(lambda q, cols: t[2, q, :, cols], 1, 0, 3, True)
 
     @even
     def _():
@@ -230,10 +238,6 @@
         cr_g.wait_recv()
         pair(lambda q, cols: t[2, q, :, cols], 1, 3, 3, True)
 
-    @odd
-    def _():
-        pair(lambda q, cols: t[2, q, :, cols], 1, 0, 3, True)
-
     gf[...] = times(wt, bx[g_up2].reshape(512, 256))
 
     @even
@@ -241,44 +245,64 @@
         out3[1] = gf[...].astype(BF)
         c_g.start()
 
-    out3[2] = (goth[...] + times(w, rg[...].reshape(512, 256))).astype(BF)
+    goth[...] = times(w, rg[...].reshape(512, 256))
+
+    @odd
+    def _():
+        gown[...] += gf[...]
+
+    sent(*ca[0])
+    for c in ca[1]:
+        c.start()
+    c_f = copy(out3.at[0], in3.at[0], up1)
+    c_x = copy(out3.at[2], in3.at[2], twin)
+    cr_f.wait_recv()
+    for c in ca[0]:
+        c.wait_recv()
+    pair(lambda q, cols: t[0, q, :, cols], 0, 2, 2, True)
+    gown[...] += times(w, rf[...].reshape(512, 256))
+    gf[...] = times(wt, bo[g_up1].reshape(512, 256))
+
+    @even
+    def _():
+        c_g.wait_recv()
+        gf[...] += in3[1].astype(F32)
+
+    for c in ca[1]:
+        c.wait_recv()
+    pair(lambda q, cols: t[1, q, :, cols], 1, 2, 1, True)
+    out3[0] = (gf[...] + times(wt, bx[g_up1].reshape(512, 256))).astype(BF)
+    c_f.start()
+    out3[2] = (goth[...] + times(w, rf[...].reshape(512, 256))).astype(BF)
     c_x.start()
 
     lane = lax.broadcasted_iota(jnp.int32, (8, 128), 1)
     total = [-jnp.sum(esum[n, 0:1], axis=1, keepdims=True) for n in range(4)]
     first_at = 1 + 2 * k
     en[0] = jnp.where(lane == first_at, total[1], jnp.where(lane == 4 - first_at, total[3], 0.0))
+    c_e = copy(en.at[0], en.at[1], twin)
     c_e.start()
     kept = jnp.where(lane == 0, total[0], jnp.where(lane == 2, total[2], 0.0))
     c_e.wait_recv()
     energy_ref[...] = (kept + en[1])[0:1, 0:4]
 
-    @odd
-    def _():
-        gown[...] += gf[...]
-
     c_x.wait_recv()
     gown[...] += in3[2].astype(F32)
     c_f.wait_recv()
     gown[...] += in3[0].astype(F32)
 
-    @even
-    def _():
-        c_g.wait_recv()
-        gown[...] += in3[1].astype(F32)
-
     for n in range(4):
         gamma_ref[:, 128 * n:128 * n + 128] = gown[128 * n:128 * n + 128].T
 
-    only_even = [cg_near, cr_g, c_g] + cg_far + ca[2]
-    for c in used:
-        if all(c is not e for e in only_even):
+    for c, only_even in used:
+        if not only_even and all(c is not d for d in done):
             c.wait_send()
 
     @even
     def _():
-        for c in only_even:
-            c.wait_send()
+        for c, only_even in used:
+            if only_even and all(c is not d for d in done):
+                c.wait_send()
 
 
 def per_device(factors, occ_energy, vir_energy):

time: 93 us -> 90.5 us (0.973)
  the two profiles are of different devices: /device:TPU:8 before, /device:TPU:6 now
where the time goes in v2:
time: 90.5 us; the launch traced here: 88.9 us
  Pallas kernels  84.1 us (93%)
  local copies, waits for them, and re-layouts  3.47 us (4%)
  between operations  1.29 us (1%)
    pallas_call x1, Pallas kernels, per_device(): pl.pallas_call(kernel, out_shape=(jax.ShapeDtypeStruct((256, 512), F32),...  84.1 us
    unnamed x6, local copies, waits for them, and re-layouts  3.47 us

profile of v2, /device:TPU:6, one launch (start us, length us, event | category | flops | bytes accessed | tf_op | source)
XLA Modules:
  0.0 88.9 jit_solution(8463345639412338189)
XLA Ops:
  1.3 0.0 copy-start.1
  1.3 0.7 copy-done.1
  2.0 0.0 copy-start
  2.0 0.9 %copy-done = bf16[256,1,512]{2,0,1:T(8,128)(2,1)S(1)} copy-done((bf16[256,1,512]{2,0,1:T(8,128)(2,1)S(1)}, bf16[256,1,512]{2,0,1:T(8,128)(2,1)}, u32[]{:S(2)}) %copy-start) | copy-done | bytes 262168
  2.9 84.1 %pairs.1 = (f32[256,512]{1,0:T(8,128)S(1)}, f32[1,4]{1,0:T(1,128)S(1)}) custom-call(bf16[256,512]{1,0:T(8,128)(2,1)S(1)} %bitcast.4, f32[1]{0:T(128)S(6)} %copy.7.occ_ref, f32[1,512]{1,0:T(1,128)S(1)} %bitcast.5), custom_call_target="tpu_custom_call" | custom-call | tf_op jit(solution)/shard_map/pairs/pallas_call | solution.py:310
  87.0 1.3 %copy.5 = f32[256,1,512]{2,1,0:T(1,128)} copy(f32[256,1,512]{2,0,1:T(8,128)S(1)} %bitcast.3) | data formatting | bytes 1048576
  88.4 0.5 copy.8
Async XLA Ops:
  1.3 0.7 copy-start.1
  2.0 0.9 %copy-start = (bf16[256,1,512]{2,0,1:T(8,128)(2,1)S(1)}, bf16[256,1,512]{2,0,1:T(8,128)(2,1)}, u32[]{:S(2)}) copy-start(bf16[256,1,512]{2,0,1:T(8,128)(2,1)} %param.3) | copy-start | bytes 786436

commit v3 on v2

--- a/solution.py
+++ b/solution.py
@@ -11,7 +11,7 @@
 NX = 4
 NU = 64
 HALF = NU // 2
-COPIES = 72
+COPIES = 96
 
 
 def place(x, u, k):
@@ -25,7 +25,7 @@
 
 def kernel(
     f_ref, occ_ref, vir_ref, gamma_ref, energy_ref,
-    bo, bx, sf, sg, rf, rg, t, a0, vv, acc, acc2, w, wt,
+    bo, bx, sf, sg, sv, rf, rg, t, a0, vv, acc, acc2, w, wt,
     gown, goth, gf, out3, in3, eps, esum, en, send, recv,
 ):
     b = lax.axis_index("blk")
@@ -47,24 +47,43 @@
     h_down1 = lax.div(lax.rem(u + NU - 1, NU), HALF)
     h_down2 = lax.div(lax.rem(u + NU - 2, NU), HALF)
     g_up1 = NX * lax.div(lax.rem(u + 1, NU), HALF) + x
+    h_up1 = lax.div(lax.rem(u + 1, NU), HALF)
     g_up2 = (1 - k) * (NX * lax.div(lax.rem(u + 2, NU), HALF) + x) + k * g
     mine = pl.ds(pl.multiple_of(32 * x, 32), 32)
 
     barrier = pltpu.get_barrier_semaphore()
-    others = xs + [partner, twin, down1, down2, up1, up2]
+    detour, undetour = place(x, u + 3, k), place(x, u + NU - 3, k)
+    down4, up4 = place(x, u + NU - 4, k), place(x, u + 4, k)
+    others = xs + [partner, twin, down1, down2, up1, up2, detour, undetour, down4, up4]
     for device in others:
         pl.semaphore_signal(barrier, inc=1, device_id=device, device_id_type=MESH)
 
+    who = {
+        "all": None,
+        "even": k == 0,
+        "skip": (k == 0) & (y == 1),
+        "relay": (k == 0) & (y > 0),
+        "direct": (k == 0) | (y > 0),
+        "detour": (k == 1) & (y == 0),
+        "detoured": (k == 1) & (y == 3),
+    }
     used, done = [], []
 
-    def copy(src, dst, device, only_even=False):
+    def copy(src, dst, device, sender="all", lands_as=None):
         n = len(used)
         made = pltpu.make_async_remote_copy(
-            src_ref=src, dst_ref=dst, send_sem=send.at[n], recv_sem=recv.at[n],
+            src_ref=src, dst_ref=dst, send_sem=send.at[n],
+            recv_sem=recv.at[n if lands_as is None else slot_of[id(lands_as)]],
             device_id=device, device_id_type=MESH,
         )
-        used.append((made, only_even))
+        slot_of[id(made)] = n
+        used.append((made, sender))
         return made
+
+    slot_of = {}
+
+    def only(sender, body):
+        pl.when(who[sender])(body)
 
     def sent(*copies):
         for c in copies:
@@ -91,22 +110,54 @@
     cx = [copy(bo.at[g], bo.at[g], xs[d]) for d in range(3)]
     ce = [copy(eps.at[0], eps.at[n], device) for n, device in ((1, twin), (2, down1), (3, down2))]
     cr_f = copy(bo.at[NX * h_down1 + x], rf, down1)
-    cr_g = copy(bo.at[NX * h_down2 + x], rg, down2, True)
+    cr_g = copy(bo.at[NX * h_down2 + x], rg, down2, "even")
     for c in cz[:2] + cx + ce:
         c.start()
     pl.when(y > 0)(cr_f.start)
     pl.when((y > 1) & (k == 0))(cr_g.start)
     near4, far4 = pl.ds(near, NX), pl.ds(far, NX)
+    up_near4 = pl.ds(NX * h_up1, NX)
+    up_far4 = pl.ds(NX - NX * h_up1, NX)
     ct_near = copy(bo.at[near4], bx.at[near4], twin)
-    cf_near = copy(bo.at[near4, :, mine], sf.at[near4], down1)
-    cg_near = copy(bo.at[near4, :, mine], sg.at[near4], down2, True)
+
+    def slices(groups, up_groups, q):
+        own = bo.at[groups, q, mine]
+        f = copy(own, sf.at[groups, q], down1, "direct")
+        f_out = copy(own, sv.at[groups, q], detour, "detour")
+        f_in = copy(sv.at[groups, q], sf.at[groups, q], down4, "detoured", f)
+        g = copy(own, sg.at[groups, q], down2, "skip")
+        g_in = copy(sf.at[up_groups, q], sg.at[up_groups, q], down1, "relay", g)
+
+        def first():
+            only("direct", f.start)
+            only("detour", f_out.start)
+            only("skip", g.start)
+
+        def second():
+            @pl.when(who["detoured"])
+            def _():
+                f_out.wait_recv()
+                f_in.start()
+
+            @even
+            def _():
+                f.wait_recv()
+
+            only("relay", g_in.start)
+
+        def last():
+            odd(f.wait_recv)
+            even(g.wait_recv)
+
+        return first, second, last
+
+    to_near = slices(near4, up_near4, slice(None))
     sent(cz[0])
     cz[2].start()
     for c in cx:
         c.wait_recv()
     ct_near.start()
-    cf_near.start()
-    even(cg_near.start)
+    to_near[0]()
     sent(cz[1])
     cz[3].start()
 
@@ -121,32 +172,32 @@
             dst[:, cols] = total if init else dst[:, cols] + total
 
     gram(acc, bo, bo, near, True)
+    to_near[1]()
     ct_near.wait_recv()
     odd(lambda: gram(acc2, bo, bx, near, True))
 
     cxf = [[copy(bo.at[gfar, q], bo.at[gfar, q], xs[d]) for d in range(3)] for q in range(4)]
     ct_far = [copy(bo.at[far4, q], bx.at[far4, q], twin) for q in range(4)]
-    cf_far = [copy(bo.at[far4, q, mine], sf.at[far4, q], down1) for q in range(4)]
-    cg_far = [copy(bo.at[far4, q, mine], sg.at[far4, q], down2, True) for q in range(4)]
-    for q in range(5):
-        if q < 4:
-            cz[q].wait_recv()
-            for c in cxf[q]:
+    to_far = [slices(far4, up_far4, q) for q in range(4)]
+    for step in range(6):
+        if step < 4:
+            cz[step].wait_recv()
+            for c in cxf[step]:
                 c.start()
-        if q > 0:
-            for c in cxf[q - 1]:
+        if 1 <= step < 5:
+            for c in cxf[step - 1]:
                 c.wait_recv()
-            cf_far[q - 1].start()
-            even(cg_far[q - 1].start)
-            ct_far[q - 1].start()
+            to_far[step - 1][0]()
+            ct_far[step - 1].start()
+        if step >= 2:
+            to_far[step - 2][1]()
     pl.when(y == 0)(cr_f.start)
     pl.when((y < 2) & (k == 0))(cr_g.start)
 
-    for c in ce[:2]:
+    for c in ce + ct_far:
         c.wait_recv()
-    ce[2].wait_recv()
-    for c in [cf_near] + cf_far + ct_far:
-        c.wait_recv()
+    for part in [to_near] + to_far:
+        part[2]()
 
     def amplitude(integral, first, second, q, rows):
         gap = vv[q, rows] - eps[first, 0:1, :] - eps[second, 0:1, :]
@@ -165,24 +216,21 @@
         for q in range(4):
             t[p, q, mine] = amplitude(total[32 * q:32 * q + 32], first, second, q, mine)
 
-    ca = [[copy(t.at[p, :, mine], t.at[p, :, mine], xs[d], p == 2) for d in range(3)] for p in range(3)]
+    ca = [[copy(t.at[p, :, mine], t.at[p, :, mine], xs[d], "even" if p == 2 else "all") for d in range(3)] for p in range(3)]
+
+    def begin(copies):
+        for c in copies:
+            c.start()
 
     @even
     def _():
-        for c in [cg_near] + cg_far:
-            c.wait_recv()
         sliced(2, sg, bx, 1, 3)
-        for c in ca[2]:
-            c.start()
+        begin(ca[2])
 
     sliced(0, sf, bo, 0, 2)
-
-    @odd
-    def _():
-        for c in ca[0]:
-            c.start()
-
+    begin(ca[0])
     sliced(1, sf, bx, 1, 2)
+    odd(lambda: begin(ca[1]))
 
     def pair(read, first, second, slot, both):
         @pl.loop(0, 4)
@@ -211,14 +259,13 @@
     def _():
         for c in ca[2]:
             c.wait_send()
-        for c in ca[0]:
-            c.start()
+        begin(ca[1])
     done.extend(ca[2])
 
     pair(lambda q, cols: a0[q, :, cols], 0, 0, 0, False)
     gown[...] = times(w, bo[g].reshape(512, 256))
 
-    c_g = copy(out3.at[1], in3.at[1], up1, True)
+    c_g = copy(out3.at[1], in3.at[1], up1, "even")
 
     @odd
     def _():
@@ -251,9 +298,6 @@
     def _():
         gown[...] += gf[...]
 
-    sent(*ca[0])
-    for c in ca[1]:
-        c.start()
     c_f = copy(out3.at[0], in3.at[0], up1)
     c_x = copy(out3.at[2], in3.at[2], twin)
     cr_f.wait_recv()
@@ -294,15 +338,13 @@
     for n in range(4):
         gamma_ref[:, 128 * n:128 * n + 128] = gown[128 * n:128 * n + 128].T
 
-    for c, only_even in used:
-        if not only_even and all(c is not d for d in done):
-            c.wait_send()
-
-    @even
-    def _():
-        for c, only_even in used:
-            if only_even and all(c is not d for d in done):
+    for name, sender in who.items():
+        left = [c for c, n in used if n == name and all(c is not d for d in done)]
+
+        def finish(left=left):
+            for c in left:
                 c.wait_send()
+        finish() if sender is None else pl.when(sender)(finish)
 
 
 def per_device(factors, occ_energy, vir_energy):
@@ -318,6 +360,7 @@
         scratch_shapes=[
             pltpu.VMEM((8, 4, 128, 256), BF),
             pltpu.VMEM((8, 4, 128, 256), BF),
+            pltpu.VMEM((8, 4, 32, 256), BF),
             pltpu.VMEM((8, 4, 32, 256), BF),
             pltpu.VMEM((8, 4, 32, 256), BF),
             pltpu.VMEM((4, 128, 256), BF),

time: 90.5 us -> 93.4 us (1.032)
  Pallas kernels: 84.1 us -> 87.1 us
    pallas_call x1, Pallas kernels: 84.1 us -> 87.1 us  [per_device(): pl.pallas_call(kernel, out_shape=(jax.ShapeDtypeStruct((256, 512), F32),...]
where the time goes in v3:
time: 93.4 us; the launch traced here: 91.8 us
  Pallas kernels  87.1 us (93%)
  local copies, waits for them, and re-layouts  3.47 us (4%)
  between operations  1.29 us (1%)
    pallas_call x1, Pallas kernels, per_device(): pl.pallas_call(kernel, out_shape=(jax.ShapeDtypeStruct((256, 512), F32),...  87.1 us
    unnamed x6, local copies, waits for them, and re-layouts  3.47 us

profile of v3, /device:TPU:6, one launch (start us, length us, event | category | flops | bytes accessed | tf_op | source)
XLA Modules:
  0.0 91.8 jit_solution(11393499991901493413)
XLA Ops:
  1.3 0.0 copy-start.1
  1.3 0.7 copy-done.1
  2.0 0.0 copy-start
  2.0 0.9 %copy-done = bf16[256,1,512]{2,0,1:T(8,128)(2,1)S(1)} copy-done((bf16[256,1,512]{2,0,1:T(8,128)(2,1)S(1)}, bf16[256,1,512]{2,0,1:T(8,128)(2,1)}, u32[]{:S(2)}) %copy-start) | copy-done | bytes 262168
  2.9 87.1 %pairs.1 = (f32[256,512]{1,0:T(8,128)S(1)}, f32[1,4]{1,0:T(1,128)S(1)}) custom-call(bf16[256,512]{1,0:T(8,128)(2,1)S(1)} %bitcast.4, f32[1]{0:T(128)S(6)} %copy.7.occ_ref, f32[1,512]{1,0:T(1,128)S(1)} %bitcast.5), custom_call_target="tpu_custom_call" | custom-call | tf_op jit(solution)/shard_map/pairs/pallas_call | solution.py:352
  90.0 1.3 %copy.5 = f32[256,1,512]{2,1,0:T(1,128)} copy(f32[256,1,512]{2,0,1:T(8,128)S(1)} %bitcast.3) | data formatting | bytes 1048576
  91.3 0.5 copy.8
Async XLA Ops:
  1.3 0.7 copy-start.1
  2.0 0.9 %copy-start = (bf16[256,1,512]{2,0,1:T(8,128)(2,1)S(1)}, bf16[256,1,512]{2,0,1:T(8,128)(2,1)}, u32[]{:S(2)}) copy-start(bf16[256,1,512]{2,0,1:T(8,128)(2,1)} %param.3) | copy-start | bytes 786436

commit v4 on v3

--- a/solution.py
+++ b/solution.py
@@ -11,7 +11,7 @@
 NX = 4
 NU = 64
 HALF = NU // 2
-COPIES = 96
+COPIES = 112
 
 
 def place(x, u, k):
@@ -61,8 +61,8 @@
     who = {
         "all": None,
         "even": k == 0,
-        "skip": (k == 0) & (y == 1),
-        "relay": (k == 0) & (y > 0),
+        "skip": (k == 0) & (y > 0),
+        "relay": (k == 0) & (y == 3),
         "direct": (k == 0) | (y > 0),
         "detour": (k == 1) & (y == 0),
         "detoured": (k == 1) & (y == 3),
@@ -106,7 +106,10 @@
 
     pl.semaphore_wait(barrier, len(others))
 
-    cz = [copy(bo.at[g, q], bo.at[g, q], partner) for q in range(4)]
+    def chunk(group, c):
+        return bo.at[group, c // 2, pl.ds(64 * (c % 2), 64)]
+
+    cz = [copy(chunk(g, c), chunk(g, c), partner) for c in range(8)]
     cx = [copy(bo.at[g], bo.at[g], xs[d]) for d in range(3)]
     ce = [copy(eps.at[0], eps.at[n], device) for n, device in ((1, twin), (2, down1), (3, down2))]
     cr_f = copy(bo.at[NX * h_down1 + x], rf, down1)
@@ -139,27 +142,29 @@
                 f_out.wait_recv()
                 f_in.start()
 
-            @even
+        def third():
+            @pl.when(who["relay"])
             def _():
                 f.wait_recv()
-
-            only("relay", g_in.start)
+                g_in.start()
 
         def last():
-            odd(f.wait_recv)
+            pl.when((k == 1) | (y < 3))(f.wait_recv)
             even(g.wait_recv)
 
-        return first, second, last
+        return first, second, third, last
 
     to_near = slices(near4, up_near4, slice(None))
-    sent(cz[0])
-    cz[2].start()
+    for n in range(3):
+        sent(cz[n])
+        cz[n + 2].start()
     for c in cx:
         c.wait_recv()
     ct_near.start()
     to_near[0]()
-    sent(cz[1])
-    cz[3].start()
+    for n in range(3, 6):
+        sent(cz[n])
+        cz[n + 2].start()
 
     def gram(dst, lhs, rhs, base, init):
         @pl.loop(0, 2)
@@ -176,28 +181,32 @@
     ct_near.wait_recv()
     odd(lambda: gram(acc2, bo, bx, near, True))
 
-    cxf = [[copy(bo.at[gfar, q], bo.at[gfar, q], xs[d]) for d in range(3)] for q in range(4)]
+    cxf = [[copy(chunk(gfar, c), chunk(gfar, c), xs[d]) for d in range(3)] for c in range(8)]
     ct_far = [copy(bo.at[far4, q], bx.at[far4, q], twin) for q in range(4)]
     to_far = [slices(far4, up_far4, q) for q in range(4)]
-    for step in range(6):
-        if step < 4:
+    for step in range(9):
+        if step < 8:
             cz[step].wait_recv()
             for c in cxf[step]:
                 c.start()
-        if 1 <= step < 5:
+        if step > 0:
             for c in cxf[step - 1]:
                 c.wait_recv()
-            to_far[step - 1][0]()
-            ct_far[step - 1].start()
-        if step >= 2:
-            to_far[step - 2][1]()
+        if step > 0 and step % 2 == 0:
+            to_far[step // 2 - 1][0]()
+            ct_far[step // 2 - 1].start()
+        if step > 1 and step % 2 == 1:
+            to_far[step // 2 - 1][1]()
+    to_far[3][1]()
+    for part in [to_near] + to_far:
+        part[2]()
     pl.when(y == 0)(cr_f.start)
     pl.when((y < 2) & (k == 0))(cr_g.start)
 
     for c in ce + ct_far:
         c.wait_recv()
     for part in [to_near] + to_far:
-        part[2]()
+        part[3]()
 
     def amplitude(integral, first, second, q, rows):
         gap = vv[q, rows] - eps[first, 0:1, :] - eps[second, 0:1, :]

time: 93.4 us -> 95.1 us (1.018)
  the two profiles are of different devices: /device:TPU:6 before, /device:TPU:36 now
where the time goes in v4:
time: 95.1 us; the launch traced here: 94.9 us
  Pallas kernels  90.2 us (95%)
  local copies, waits for them, and re-layouts  3.47 us (4%)
  between operations  1.29 us (1%)
    pallas_call x1, Pallas kernels, per_device(): pl.pallas_call(kernel, out_shape=(jax.ShapeDtypeStruct((256, 512), F32),...  90.2 us
    unnamed x6, local copies, waits for them, and re-layouts  3.47 us

profile of v4, /device:TPU:36, one launch (start us, length us, event | category | flops | bytes accessed | tf_op | source)
XLA Modules:
  0.0 94.9 jit_solution(2067289499706278671)
XLA Ops:
  1.3 0.0 copy-start.1
  1.3 0.7 copy-done.1
  2.0 0.0 copy-start
  2.0 0.9 copy-done
  2.9 90.2 %pairs.1 = (f32[256,512]{1,0:T(8,128)S(1)}, f32[1,4]{1,0:T(1,128)S(1)}) custom-call(bf16[256,512]{1,0:T(8,128)(2,1)S(1)} %bitcast.4, f32[1]{0:T(128)S(6)} %copy.7.occ_ref, f32[1,512]{1,0:T(1,128)S(1)} %bitcast.5), custom_call_target="tpu_custom_call" | custom-call | tf_op jit(solution)/shard_map/pairs/pallas_call | solution.py:361
  93.1 1.3 %copy.5 = f32[256,1,512]{2,1,0:T(1,128)} copy(f32[256,1,512]{2,0,1:T(8,128)S(1)} %bitcast.3) | data formatting | bytes 1048576
  94.4 0.5 copy.8
Async XLA Ops:
  1.3 0.7 copy-start.1
  2.0 0.9 %copy-start = (bf16[256,1,512]{2,0,1:T(8,128)(2,1)S(1)}, bf16[256,1,512]{2,0,1:T(8,128)(2,1)}, u32[]{:S(2)}) copy-start(bf16[256,1,512]{2,0,1:T(8,128)(2,1)} %param.3) | copy-start | bytes 786436

commit v5 on v3

--- a/solution.py
+++ b/solution.py
@@ -11,7 +11,7 @@
 NX = 4
 NU = 64
 HALF = NU // 2
-COPIES = 96
+COPIES = 128
 
 
 def place(x, u, k):
@@ -47,8 +47,7 @@
     h_down1 = lax.div(lax.rem(u + NU - 1, NU), HALF)
     h_down2 = lax.div(lax.rem(u + NU - 2, NU), HALF)
     g_up1 = NX * lax.div(lax.rem(u + 1, NU), HALF) + x
-    h_up1 = lax.div(lax.rem(u + 1, NU), HALF)
-    g_up2 = (1 - k) * (NX * lax.div(lax.rem(u + 2, NU), HALF) + x) + k * g
+    g_up2 = NX * lax.div(lax.rem(u + 2, NU), HALF) + x
     mine = pl.ds(pl.multiple_of(32 * x, 32), 32)
 
     barrier = pltpu.get_barrier_semaphore()
@@ -61,8 +60,9 @@
     who = {
         "all": None,
         "even": k == 0,
-        "skip": (k == 0) & (y == 1),
-        "relay": (k == 0) & (y > 0),
+        "skip": (k == 0) & (y > 0),
+        "round": (k == 0) & (y == 0),
+        "rounded": (k == 0) & (y == 2),
         "direct": (k == 0) | (y > 0),
         "detour": (k == 1) & (y == 0),
         "detoured": (k == 1) & (y == 3),
@@ -106,7 +106,11 @@
 
     pl.semaphore_wait(barrier, len(others))
 
-    cz = [copy(bo.at[g, q], bo.at[g, q], partner) for q in range(4)]
+    def chunk(group, c):
+        q, first, rows = ((0, 0, 128), (1, 0, 128), (2, 0, 128), (3, 0, 64), (3, 64, 64))[c]
+        return bo.at[group, q, pl.ds(first, rows)]
+
+    cz = [copy(chunk(g, c), chunk(g, c), partner) for c in range(5)]
     cx = [copy(bo.at[g], bo.at[g], xs[d]) for d in range(3)]
     ce = [copy(eps.at[0], eps.at[n], device) for n, device in ((1, twin), (2, down1), (3, down2))]
     cr_f = copy(bo.at[NX * h_down1 + x], rf, down1)
@@ -116,22 +120,23 @@
     pl.when(y > 0)(cr_f.start)
     pl.when((y > 1) & (k == 0))(cr_g.start)
     near4, far4 = pl.ds(near, NX), pl.ds(far, NX)
-    up_near4 = pl.ds(NX * h_up1, NX)
-    up_far4 = pl.ds(NX - NX * h_up1, NX)
     ct_near = copy(bo.at[near4], bx.at[near4], twin)
 
-    def slices(groups, up_groups, q):
+    def slices(groups, q):
         own = bo.at[groups, q, mine]
+        there = sv.at[groups, q]
         f = copy(own, sf.at[groups, q], down1, "direct")
-        f_out = copy(own, sv.at[groups, q], detour, "detour")
-        f_in = copy(sv.at[groups, q], sf.at[groups, q], down4, "detoured", f)
+        f_out = copy(own, there, detour, "detour")
+        f_in = copy(there, sf.at[groups, q], down4, "detoured", f)
         g = copy(own, sg.at[groups, q], down2, "skip")
-        g_in = copy(sf.at[up_groups, q], sg.at[up_groups, q], down1, "relay", g)
+        g_out = copy(own, there, up2, "round")
+        g_in = copy(there, sg.at[groups, q], down4, "rounded", g)
 
         def first():
             only("direct", f.start)
             only("detour", f_out.start)
             only("skip", g.start)
+            only("round", g_out.start)
 
         def second():
             @pl.when(who["detoured"])
@@ -139,19 +144,14 @@
                 f_out.wait_recv()
                 f_in.start()
 
-            @even
+            @pl.when(who["rounded"])
             def _():
-                f.wait_recv()
-
-            only("relay", g_in.start)
-
-        def last():
-            odd(f.wait_recv)
-            even(g.wait_recv)
-
-        return first, second, last
-
-    to_near = slices(near4, up_near4, slice(None))
+                g_out.wait_recv()
+                g_in.start()
+
+        return first, second, f, g
+
+    to_near = slices(near4, slice(None))
     sent(cz[0])
     cz[2].start()
     for c in cx:
@@ -160,6 +160,7 @@
     to_near[0]()
     sent(cz[1])
     cz[3].start()
+    cz[4].start()
 
     def gram(dst, lhs, rhs, base, init):
         @pl.loop(0, 2)
@@ -176,61 +177,77 @@
     ct_near.wait_recv()
     odd(lambda: gram(acc2, bo, bx, near, True))
 
-    cxf = [[copy(bo.at[gfar, q], bo.at[gfar, q], xs[d]) for d in range(3)] for q in range(4)]
+    cxf = [[copy(chunk(gfar, c), chunk(gfar, c), xs[d]) for d in range(3)] for c in range(5)]
     ct_far = [copy(bo.at[far4, q], bx.at[far4, q], twin) for q in range(4)]
-    to_far = [slices(far4, up_far4, q) for q in range(4)]
+    to_far = [slices(far4, q) for q in range(4)]
     for step in range(6):
-        if step < 4:
+        if step < 5:
             cz[step].wait_recv()
             for c in cxf[step]:
                 c.start()
-        if 1 <= step < 5:
+        if step > 0:
             for c in cxf[step - 1]:
                 c.wait_recv()
-            to_far[step - 1][0]()
-            ct_far[step - 1].start()
-        if step >= 2:
+        if step in (1, 2, 3, 5):
+            q = min(step, 4) - 1
+            to_far[q][0]()
+            ct_far[q].start()
+        if step in (2, 3, 4):
             to_far[step - 2][1]()
+    to_far[3][1]()
     pl.when(y == 0)(cr_f.start)
     pl.when((y < 2) & (k == 0))(cr_g.start)
 
-    for c in ce + ct_far:
-        c.wait_recv()
-    for part in [to_near] + to_far:
-        part[2]()
-
-    def amplitude(integral, first, second, q, rows):
-        gap = vv[q, rows] - eps[first, 0:1, :] - eps[second, 0:1, :]
+    def amplitude(integral, first, second, q, rows, cols=slice(None)):
+        gap = vv[q, rows, cols] - eps[first, 0:1, cols] - eps[second, 0:1, cols]
         return (-integral / gap).astype(BF)
 
-    def sliced(p, piece, whole, first, second):
+    def tile(piece, pq, whole, wq):
         halves = []
         for half in range(2):
             total = None
             for n in range(NX):
-                group = NX * half + n
-                part = nt(piece[group].reshape(128, 256), whole[group].reshape(512, 256))
+                lhs, rhs = piece[NX * half + n, pq], whole[NX * half + n, wq]
+                part = nt(lhs.reshape(-1, 256), rhs.reshape(-1, 256))
                 total = part if total is None else total + part
             halves.append(total)
-        total = halves[0] + halves[1]
-        for q in range(4):
-            t[p, q, mine] = amplitude(total[32 * q:32 * q + 32], first, second, q, mine)
-
-    ca = [[copy(t.at[p, :, mine], t.at[p, :, mine], xs[d], "even" if p == 2 else "all") for d in range(3)] for p in range(3)]
+        return halves[0] + halves[1]
+
+    head, tail = slice(0, 384), slice(384, 512)
+    early = [[copy(t.at[p, 0:3, mine, head], t.at[p, 0:3, mine, head], xs[d], "even" if p == 2 else "all")
+              for d in range(3)] for p in range(3)]
+    late = [[copy(src, src, xs[d], "even" if p == 2 else "all") for d in range(3)
+             for src in (t.at[p, 3, mine], t.at[p, 0:3, mine, tail])] for p in range(3)]
 
     def begin(copies):
         for c in copies:
             c.start()
 
+    def arrive(copies):
+        for c in copies:
+            c.wait_recv()
+
+    def first_batch(p, piece, whole, first, second):
+        total = tile(piece, slice(0, 3), whole, slice(0, 3))
+        for q in range(3):
+            t[p, q, mine, head] = amplitude(total[32 * q:32 * q + 32], first, second, q, mine, head)
+        begin(early[p])
+
+    def second_batch(p, piece, whole, first, second):
+        t[p, 3, mine] = amplitude(tile(piece, slice(3, 4), whole, slice(0, 4)), first, second, 3, mine)
+        total = tile(piece, slice(0, 3), whole, slice(3, 4))
+        for q in range(3):
+            t[p, q, mine, tail] = amplitude(total[32 * q:32 * q + 32], first, second, q, mine, tail)
+        begin(late[p])
+
+    arrive(ce + [to_near[2]] + [part[2] for part in to_far[:3]] + ct_far[:3])
+    first_batch(0, sf, bo, 0, 2)
+    first_batch(1, sf, bx, 1, 2)
+
     @even
     def _():
-        sliced(2, sg, bx, 1, 3)
-        begin(ca[2])
-
-    sliced(0, sf, bo, 0, 2)
-    begin(ca[0])
-    sliced(1, sf, bx, 1, 2)
-    odd(lambda: begin(ca[1]))
+        arrive([to_near[3]] + [part[3] for part in to_far[:3]])
+        first_batch(2, sg, bx, 1, 3)
 
     def pair(read, first, second, slot, both):
         @pl.loop(0, 4)
@@ -255,17 +272,17 @@
         rows = pl.ds(pl.multiple_of(128 * q, 128), 128)
         a0[q] = amplitude(acc[rows], 0, 0, q, slice(None))
 
-    @even
-    def _():
-        for c in ca[2]:
-            c.wait_send()
-        begin(ca[1])
-    done.extend(ca[2])
-
     pair(lambda q, cols: a0[q, :, cols], 0, 0, 0, False)
     gown[...] = times(w, bo[g].reshape(512, 256))
 
-    c_g = copy(out3.at[1], in3.at[1], up1, "even")
+    arrive([to_far[3][2], ct_far[3]])
+    second_batch(0, sf, bo, 0, 2)
+    second_batch(1, sf, bx, 1, 2)
+
+    @even
+    def _():
+        to_far[3][3].wait_recv()
+        second_batch(2, sg, bx, 1, 3)
 
     @odd
     def _():
@@ -275,50 +292,39 @@
         def _(q):
             rows = pl.ds(pl.multiple_of(128 * q, 128), 128)
             t[2, q] = amplitude(acc2[rows], 1, 0, q, slice(None))
-        rg[...] = bo[g]
         pair(lambda q, cols: t[2, q, :, cols], 1, 0, 3, True)
-
-    @even
-    def _():
-        for c in ca[2]:
-            c.wait_recv()
-        cr_g.wait_recv()
-        pair(lambda q, cols: t[2, q, :, cols], 1, 3, 3, True)
-
-    gf[...] = times(wt, bx[g_up2].reshape(512, 256))
-
-    @even
-    def _():
-        out3[1] = gf[...].astype(BF)
-        c_g.start()
-
-    goth[...] = times(w, rg[...].reshape(512, 256))
-
-    @odd
-    def _():
-        gown[...] += gf[...]
+        gown[...] += times(wt, bx[g].reshape(512, 256))
+        goth[...] = times(w, bo[g].reshape(512, 256))
 
     c_f = copy(out3.at[0], in3.at[0], up1)
+    c_g = copy(out3.at[1], in3.at[1], up2, "even")
     c_x = copy(out3.at[2], in3.at[2], twin)
     cr_f.wait_recv()
-    for c in ca[0]:
-        c.wait_recv()
+    arrive(early[0] + late[0])
     pair(lambda q, cols: t[0, q, :, cols], 0, 2, 2, True)
+    gf[...] = times(wt, bo[g_up1].reshape(512, 256))
     gown[...] += times(w, rf[...].reshape(512, 256))
-    gf[...] = times(wt, bo[g_up1].reshape(512, 256))
-
-    @even
-    def _():
-        c_g.wait_recv()
-        gf[...] += in3[1].astype(F32)
-
-    for c in ca[1]:
-        c.wait_recv()
+    arrive(early[1] + late[1])
     pair(lambda q, cols: t[1, q, :, cols], 1, 2, 1, True)
     out3[0] = (gf[...] + times(wt, bx[g_up1].reshape(512, 256))).astype(BF)
     c_f.start()
-    out3[2] = (goth[...] + times(w, rf[...].reshape(512, 256))).astype(BF)
-    c_x.start()
+    part = times(w, rf[...].reshape(512, 256))
+
+    @odd
+    def _():
+        out3[2] = (goth[...] + part).astype(BF)
+        c_x.start()
+
+    @even
+    def _():
+        goth[...] = part
+        cr_g.wait_recv()
+        arrive(early[2] + late[2])
+        pair(lambda q, cols: t[2, q, :, cols], 1, 3, 3, True)
+        out3[1] = times(wt, bx[g_up2].reshape(512, 256)).astype(BF)
+        c_g.start()
+        out3[2] = (goth[...] + times(w, rg[...].reshape(512, 256))).astype(BF)
+        c_x.start()
 
     lane = lax.broadcasted_iota(jnp.int32, (8, 128), 1)
     total = [-jnp.sum(esum[n, 0:1], axis=1, keepdims=True) for n in range(4)]
@@ -334,6 +340,11 @@
     gown[...] += in3[2].astype(F32)
     c_f.wait_recv()
     gown[...] += in3[0].astype(F32)
+
+    @even
+    def _():
+        c_g.wait_recv()
+        gown[...] += in3[1].astype(F32)
 
     for n in range(4):
         gamma_ref[:, 128 * n:128 * n + 128] = gown[128 * n:128 * n + 128].T

time: 93.4 us -> 94.6 us (1.013)
  the two profiles are of different devices: /device:TPU:6 before, /device:TPU:1 now
where the time goes in v5:
time: 94.6 us; the launch traced here: 94.4 us
  Pallas kernels  89.6 us (95%)
  local copies, waits for them, and re-layouts  3.47 us (4%)
  between operations  1.29 us (1%)
    pallas_call x1, Pallas kernels, per_device(): pl.pallas_call(kernel, out_shape=(jax.ShapeDtypeStruct((256, 512), F32),...  89.6 us
    unnamed x6, local copies, waits for them, and re-layouts  3.47 us

profile of v5, /device:TPU:1, one launch (start us, length us, event | category | flops | bytes accessed | tf_op | source)
XLA Modules:
  0.0 94.4 jit_solution(8733751084832932981)
XLA Ops:
  1.3 0.0 copy-start.1
  1.3 0.7 copy-done.1
  2.0 0.0 copy-start
  2.0 0.9 %copy-done = bf16[256,1,512]{2,0,1:T(8,128)(2,1)S(1)} copy-done((bf16[256,1,512]{2,0,1:T(8,128)(2,1)S(1)}, bf16[256,1,512]{2,0,1:T(8,128)(2,1)}, u32[]{:S(2)}) %copy-start) | copy-done | bytes 262168
  2.9 89.6 %pairs.1 = (f32[256,512]{1,0:T(8,128)S(1)}, f32[1,4]{1,0:T(1,128)S(1)}) custom-call(bf16[256,512]{1,0:T(8,128)(2,1)S(1)} %bitcast.4, f32[1]{0:T(128)S(6)} %copy.7.occ_ref, f32[1,512]{1,0:T(1,128)S(1)} %bitcast.5), custom_call_target="tpu_custom_call" | custom-call | tf_op jit(solution)/shard_map/pairs/pallas_call | solution.py:363
  92.5 1.3 %copy.5 = f32[256,1,512]{2,1,0:T(1,128)} copy(f32[256,1,512]{2,0,1:T(8,128)S(1)} %bitcast.3) | data formatting | bytes 1048576
  93.9 0.5 copy.8
Async XLA Ops:
  1.3 0.7 copy-start.1
  2.0 0.9 %copy-start = (bf16[256,1,512]{2,0,1:T(8,128)(2,1)S(1)}, bf16[256,1,512]{2,0,1:T(8,128)(2,1)}, u32[]{:S(2)}) copy-start(bf16[256,1,512]{2,0,1:T(8,128)(2,1)} %param.3) | copy-start | bytes 786436

commit v6 on v5

--- a/solution.py
+++ b/solution.py
@@ -26,7 +26,7 @@
 def kernel(
     f_ref, occ_ref, vir_ref, gamma_ref, energy_ref,
     bo, bx, sf, sg, sv, rf, rg, t, a0, vv, acc, acc2, w, wt,
-    gown, goth, gf, out3, in3, eps, esum, en, send, recv,
+    gown, goth, gf, out3, in3, eps, esum, en, f_own, vir, local, send, recv,
 ):
     b = lax.axis_index("blk")
     a = lax.axis_index("aux")
@@ -51,9 +51,8 @@
     mine = pl.ds(pl.multiple_of(32 * x, 32), 32)
 
     barrier = pltpu.get_barrier_semaphore()
-    detour, undetour = place(x, u + 3, k), place(x, u + NU - 3, k)
     down4, up4 = place(x, u + NU - 4, k), place(x, u + 4, k)
-    others = xs + [partner, twin, down1, down2, up1, up2, detour, undetour, down4, up4]
+    others = xs + [partner, twin, down1, down2, up1, up2, down4, up4]
     for device in others:
         pl.semaphore_signal(barrier, inc=1, device_id=device, device_id_type=MESH)
 
@@ -63,9 +62,6 @@
         "skip": (k == 0) & (y > 0),
         "round": (k == 0) & (y == 0),
         "rounded": (k == 0) & (y == 2),
-        "direct": (k == 0) | (y > 0),
-        "detour": (k == 1) & (y == 0),
-        "detoured": (k == 1) & (y == 3),
     }
     used, done = [], []
 
@@ -96,9 +92,15 @@
     def odd(body):
         pl.when(k == 1)(body)
 
-    bo[g] = f_ref[...].T.reshape(4, 128, 256)
+    reads = [pltpu.make_async_copy(f_ref, f_own, local.at[0]), pltpu.make_async_copy(vir_ref, vir, local.at[1])]
+    for c in reads:
+        c.start()
+    for c in reads:
+        c.wait()
+
+    bo[g] = f_own[...].T.reshape(4, 128, 256)
     eps[0] = jnp.full((8, 512), occ_ref[0], F32)
-    row = jnp.broadcast_to(vir_ref[...], (128, 512))
+    row = jnp.broadcast_to(vir[...], (128, 512))
     for q in range(4):
         column = jnp.broadcast_to(row[:, 128 * q:128 * q + 128].T[:, 0:1], (128, 512))
         vv[q] = column + row
@@ -125,25 +127,17 @@
     def slices(groups, q):
         own = bo.at[groups, q, mine]
         there = sv.at[groups, q]
-        f = copy(own, sf.at[groups, q], down1, "direct")
-        f_out = copy(own, there, detour, "detour")
-        f_in = copy(there, sf.at[groups, q], down4, "detoured", f)
+        f = copy(own, sf.at[groups, q], down1)
         g = copy(own, sg.at[groups, q], down2, "skip")
         g_out = copy(own, there, up2, "round")
         g_in = copy(there, sg.at[groups, q], down4, "rounded", g)
 
         def first():
-            only("direct", f.start)
-            only("detour", f_out.start)
+            f.start()
             only("skip", g.start)
             only("round", g_out.start)
 
         def second():
-            @pl.when(who["detoured"])
-            def _():
-                f_out.wait_recv()
-                f_in.start()
-
             @pl.when(who["rounded"])
             def _():
                 g_out.wait_recv()
@@ -185,6 +179,8 @@
             cz[step].wait_recv()
             for c in cxf[step]:
                 c.start()
+        if step in (2, 3, 4):
+            to_far[step - 2][1]()
         if step > 0:
             for c in cxf[step - 1]:
                 c.wait_recv()
@@ -192,8 +188,6 @@
             q = min(step, 4) - 1
             to_far[q][0]()
             ct_far[q].start()
-        if step in (2, 3, 4):
-            to_far[step - 2][1]()
     to_far[3][1]()
     pl.when(y == 0)(cr_f.start)
     pl.when((y < 2) & (k == 0))(cr_g.start)
@@ -265,6 +259,16 @@
     def times(weight, factor):
         return jnp.dot(weight[...], factor, preferred_element_type=F32)
 
+    arrive([to_far[3][2], ct_far[3]])
+
+    @even
+    def _():
+        to_far[3][3].wait_recv()
+        second_batch(2, sg, bx, 1, 3)
+
+    second_batch(0, sf, bo, 0, 2)
+    second_batch(1, sf, bx, 1, 2)
+
     gram(acc, bo, bo, far, False)
 
     @pl.loop(0, 4)
@@ -274,15 +278,6 @@
 
     pair(lambda q, cols: a0[q, :, cols], 0, 0, 0, False)
     gown[...] = times(w, bo[g].reshape(512, 256))
-
-    arrive([to_far[3][2], ct_far[3]])
-    second_batch(0, sf, bo, 0, 2)
-    second_batch(1, sf, bx, 1, 2)
-
-    @even
-    def _():
-        to_far[3][3].wait_recv()
-        second_batch(2, sg, bx, 1, 3)
 
     @odd
     def _():
@@ -299,6 +294,16 @@
     c_f = copy(out3.at[0], in3.at[0], up1)
     c_g = copy(out3.at[1], in3.at[1], up2, "even")
     c_x = copy(out3.at[2], in3.at[2], twin)
+
+    @even
+    def _():
+        arrive(early[2] + late[2])
+        pair(lambda q, cols: t[2, q, :, cols], 1, 3, 3, True)
+        out3[1] = times(wt, bx[g_up2].reshape(512, 256)).astype(BF)
+        c_g.start()
+        cr_g.wait_recv()
+        goth[...] = times(w, rg[...].reshape(512, 256))
+
     cr_f.wait_recv()
     arrive(early[0] + late[0])
     pair(lambda q, cols: t[0, q, :, cols], 0, 2, 2, True)
@@ -308,23 +313,8 @@
     pair(lambda q, cols: t[1, q, :, cols], 1, 2, 1, True)
     out3[0] = (gf[...] + times(wt, bx[g_up1].reshape(512, 256))).astype(BF)
     c_f.start()
-    part = times(w, rf[...].reshape(512, 256))
-
-    @odd
-    def _():
-        out3[2] = (goth[...] + part).astype(BF)
-        c_x.start()
-
-    @even
-    def _():
-        goth[...] = part
-        cr_g.wait_recv()
-        arrive(early[2] + late[2])
-        pair(lambda q, cols: t[2, q, :, cols], 1, 3, 3, True)
-        out3[1] = times(wt, bx[g_up2].reshape(512, 256)).astype(BF)
-        c_g.start()
-        out3[2] = (goth[...] + times(w, rg[...].reshape(512, 256))).astype(BF)
-        c_x.start()
+    out3[2] = (goth[...] + times(w, rf[...].reshape(512, 256))).astype(BF)
+    c_x.start()
 
     lane = lax.broadcasted_iota(jnp.int32, (8, 128), 1)
     total = [-jnp.sum(esum[n, 0:1], axis=1, keepdims=True) for n in range(4)]
@@ -360,13 +350,14 @@
 
 def per_device(factors, occ_energy, vir_energy):
     vmem = pl.BlockSpec(memory_space=pltpu.VMEM)
+    hbm = pl.BlockSpec(memory_space=pl.ANY)
     gamma, energy = pl.pallas_call(
         kernel,
         out_shape=(
             jax.ShapeDtypeStruct((256, 512), F32),
             jax.ShapeDtypeStruct((1, 4), F32),
         ),
-        in_specs=[vmem, pl.BlockSpec(memory_space=pltpu.SMEM), vmem],
+        in_specs=[hbm, pl.BlockSpec(memory_space=pltpu.SMEM), hbm],
         out_specs=(vmem, vmem),
         scratch_shapes=[
             pltpu.VMEM((8, 4, 128, 256), BF),
@@ -391,11 +382,14 @@
             pltpu.VMEM((4, 8, 512), F32),
             pltpu.VMEM((4, 8, 512), F32),
             pltpu.VMEM((2, 8, 128), F32),
+            pltpu.VMEM((256, 512), BF),
+            pltpu.VMEM((1, 512), F32),
+            pltpu.SemaphoreType.DMA((2,)),
             pltpu.SemaphoreType.DMA((COPIES,)),
             pltpu.SemaphoreType.DMA((COPIES,)),
         ],
         compiler_params=pltpu.CompilerParams(
-            collective_id=0, has_side_effects=True, vmem_limit_bytes=44 << 20
+            collective_id=0, has_side_effects=True, vmem_limit_bytes=60 << 20
         ),
         name="pairs",
     )(factors.reshape(256, 512), occ_energy, vir_energy.reshape(1, 512))

time: 94.6 us -> 86.6 us (0.915)
  the two profiles are of different devices: /device:TPU:1 before, /device:TPU:6 now
where the time goes in v6:
time: 86.6 us; the launch traced here: 85.5 us
  Pallas kernels  81.3 us (94%)
  local copies, waits for them, and re-layouts  2.89 us (3%)
  between operations  1.29 us (1%)
    pallas_call x1, Pallas kernels, per_device(): pl.pallas_call(kernel, out_shape=(jax.ShapeDtypeStruct((256, 512), F32),...  81.3 us
    unnamed x4, local copies, waits for them, and re-layouts  2.89 us

profile of v6, /device:TPU:6, one launch (start us, length us, event | category | flops | bytes accessed | tf_op | source)
XLA Modules:
  0.0 85.5 jit_solution(15613370295416185980)
XLA Ops:
  1.3 81.3 %pairs.1 = (f32[256,512]{1,0:T(8,128)}, f32[1,4]{1,0:T(1,128)}) custom-call(bf16[256,512]{1,0:T(8,128)(2,1)} %bitcast.4, f32[1]{0:T(128)S(6)} %copy.7.occ_ref, f32[1,512]{1,0:T(1,128)} %bitcast.5), custom_call_target="tpu_custom_call" | custom-call | tf_op jit(solution)/shard_map/pairs/pallas_call | solution.py:354
  82.6 0.0 copy-start
  82.6 2.4 %copy.5 = f32[256,1,512]{2,1,0:T(1,128)} copy(f32[256,1,512]{2,0,1:T(8,128)} %bitcast.3) | data formatting | bytes 1048576
  85.0 0.0 copy-done
  85.0 0.5 copy.8
Async XLA Ops:
  82.6 2.4 %copy-start = (f32[1,4]{1,0:T(1,128)S(1)}, f32[1,4]{1,0:T(1,128)}, u32[]{:S(2)}) copy-start(f32[1,4]{1,0:T(1,128)} %get-tuple-element.10) | copy-start | bytes 52

commit v7 on v6

--- a/solution.py
+++ b/solution.py
@@ -25,7 +25,7 @@
 
 def kernel(
     f_ref, occ_ref, vir_ref, gamma_ref, energy_ref,
-    bo, bx, sf, sg, sv, rf, rg, t, a0, vv, acc, acc2, w, wt,
+    bo, bx, sf, sg, sv, rf, rg, t, a0, vv, acc, acc2, nacc, w, wt, tt,
     gown, goth, gf, out3, in3, eps, esum, en, f_own, vir, local, send, recv,
 ):
     b = lax.axis_index("blk")
@@ -46,8 +46,8 @@
     up1, up2 = place(x, u + 1, k), place(x, u + 2, k)
     h_down1 = lax.div(lax.rem(u + NU - 1, NU), HALF)
     h_down2 = lax.div(lax.rem(u + NU - 2, NU), HALF)
-    g_up1 = NX * lax.div(lax.rem(u + 1, NU), HALF) + x
-    g_up2 = NX * lax.div(lax.rem(u + 2, NU), HALF) + x
+    h_up1, h_up2 = lax.div(lax.rem(u + 1, NU), HALF), lax.div(lax.rem(u + 2, NU), HALF)
+    g_up1, g_up2 = NX * h_up1 + x, NX * h_up2 + x
     mine = pl.ds(pl.multiple_of(32 * x, 32), 32)
 
     barrier = pltpu.get_barrier_semaphore()
@@ -146,14 +146,14 @@
         return first, second, f, g
 
     to_near = slices(near4, slice(None))
-    sent(cz[0])
-    cz[2].start()
+    for n in range(2):
+        sent(cz[n])
+        cz[n + 2].start()
     for c in cx:
         c.wait_recv()
     ct_near.start()
     to_near[0]()
-    sent(cz[1])
-    cz[3].start()
+    sent(cz[2])
     cz[4].start()
 
     def gram(dst, lhs, rhs, base, init):
@@ -167,9 +167,31 @@
             dst[:, cols] = total if init else dst[:, cols] + total
 
     gram(acc, bo, bo, near, True)
-    to_near[1]()
     ct_near.wait_recv()
     odd(lambda: gram(acc2, bo, bx, near, True))
+
+    def tile(piece, pq, whole, wq, base):
+        total = None
+        for n in range(NX):
+            lhs, rhs = piece[base + n, pq], whole[base + n, wq]
+            part = nt(lhs.reshape(-1, 256), rhs.reshape(-1, 256))
+            total = part if total is None else total + part
+        return total
+
+    every = slice(0, 4)
+    first_1, first_2 = NX * h_up1, NX * h_up2
+    last_1, last_2 = NX - first_1, NX - first_2
+
+    def half(p, piece, whole, base):
+        nacc[p] = tile(piece, every, whole, every, base).reshape(4, 32, 512)
+
+    def halves():
+        half(0, sf, bo, first_1)
+        half(1, sf, bx, first_1)
+
+    def arrive(copies):
+        for c in copies:
+            c.wait_recv()
 
     cxf = [[copy(chunk(gfar, c), chunk(gfar, c), xs[d]) for d in range(3)] for c in range(5)]
     ct_far = [copy(bo.at[far4, q], bx.at[far4, q], twin) for q in range(4)]
@@ -179,33 +201,25 @@
             cz[step].wait_recv()
             for c in cxf[step]:
                 c.start()
-        if step in (2, 3, 4):
-            to_far[step - 2][1]()
+        if step == 3:
+            to_near[1]()
+        if step == 4:
+            to_near[2].wait_recv()
+            pl.when(h_up1 == h)(halves)
         if step > 0:
-            for c in cxf[step - 1]:
-                c.wait_recv()
+            arrive(cxf[step - 1])
         if step in (1, 2, 3, 5):
             q = min(step, 4) - 1
             to_far[q][0]()
             ct_far[q].start()
-    to_far[3][1]()
+    for part in to_far:
+        part[1]()
     pl.when(y == 0)(cr_f.start)
     pl.when((y < 2) & (k == 0))(cr_g.start)
 
     def amplitude(integral, first, second, q, rows, cols=slice(None)):
         gap = vv[q, rows, cols] - eps[first, 0:1, cols] - eps[second, 0:1, cols]
         return (-integral / gap).astype(BF)
-
-    def tile(piece, pq, whole, wq):
-        halves = []
-        for half in range(2):
-            total = None
-            for n in range(NX):
-                lhs, rhs = piece[NX * half + n, pq], whole[NX * half + n, wq]
-                part = nt(lhs.reshape(-1, 256), rhs.reshape(-1, 256))
-                total = part if total is None else total + part
-            halves.append(total)
-        return halves[0] + halves[1]
 
     head, tail = slice(0, 384), slice(384, 512)
     early = [[copy(t.at[p, 0:3, mine, head], t.at[p, 0:3, mine, head], xs[d], "even" if p == 2 else "all")
@@ -217,67 +231,85 @@
         for c in copies:
             c.start()
 
-    def arrive(copies):
-        for c in copies:
-            c.wait_recv()
-
-    def first_batch(p, piece, whole, first, second):
-        total = tile(piece, slice(0, 3), whole, slice(0, 3))
+    def first_batch(p, piece, whole, base, first, second):
+        total = tile(piece, slice(0, 3), whole, slice(0, 3), base)
         for q in range(3):
-            t[p, q, mine, head] = amplitude(total[32 * q:32 * q + 32], first, second, q, mine, head)
+            whole_sum = nacc[p, q, :, head] + total[32 * q:32 * q + 32]
+            t[p, q, mine, head] = amplitude(whole_sum, first, second, q, mine, head)
         begin(early[p])
 
-    def second_batch(p, piece, whole, first, second):
-        t[p, 3, mine] = amplitude(tile(piece, slice(3, 4), whole, slice(0, 4)), first, second, 3, mine)
-        total = tile(piece, slice(0, 3), whole, slice(3, 4))
+    def second_batch(p, piece, whole, base, first, second):
+        total = nacc[p, 3] + tile(piece, slice(3, 4), whole, every, base)
+        t[p, 3, mine] = amplitude(total, first, second, 3, mine)
+        total = tile(piece, slice(0, 3), whole, slice(3, 4), base)
         for q in range(3):
-            t[p, q, mine, tail] = amplitude(total[32 * q:32 * q + 32], first, second, q, mine, tail)
+            whole_sum = nacc[p, q, :, tail] + total[32 * q:32 * q + 32]
+            t[p, q, mine, tail] = amplitude(whole_sum, first, second, q, mine, tail)
         begin(late[p])
 
-    arrive(ce + [to_near[2]] + [part[2] for part in to_far[:3]] + ct_far[:3])
-    first_batch(0, sf, bo, 0, 2)
-    first_batch(1, sf, bx, 1, 2)
-
-    @even
-    def _():
-        arrive([to_near[3]] + [part[3] for part in to_far[:3]])
-        first_batch(2, sg, bx, 1, 3)
-
-    def pair(read, first, second, slot, both):
+    @even
+    def _():
+        to_near[3].wait_recv()
+        pl.when(h_up2 == h)(lambda: half(2, sg, bx, first_2))
+
+    gram(acc, bo, bo, far, False)
+
+    @pl.loop(0, 4)
+    def _(q):
+        rows = pl.ds(pl.multiple_of(128 * q, 128), 128)
+        a0[q] = amplitude(acc[rows], 0, 0, q, slice(None))
+
+    arrive(ce + [part[2] for part in to_far[:3]] + ct_far)
+    pl.when(h_up1 != h)(halves)
+    first_batch(0, sf, bo, last_1, 0, 2)
+    first_batch(1, sf, bx, last_1, 1, 2)
+
+    @even
+    def _():
+        arrive([part[3] for part in to_far[:3]])
+        pl.when(h_up2 != h)(lambda: half(2, sg, bx, first_2))
+        first_batch(2, sg, bx, last_2, 1, 3)
+
+    to_far[3][2].wait_recv()
+    second_batch(0, sf, bo, last_1, 0, 2)
+    second_batch(1, sf, bx, last_1, 1, 2)
+
+    @even
+    def _():
+        to_far[3][3].wait_recv()
+        second_batch(2, sg, bx, last_2, 1, 3)
+
+    def weights(p, read, both):
+        @pl.loop(0, 4)
+        def _(q):
+            rows = pl.ds(pl.multiple_of(128 * q, 128), 128)
+            turned = jnp.concatenate([read(n, rows).T for n in range(4)], axis=1)
+            tt[p, rows] = turned
+            tq, turned = read(q, slice(None)).astype(F32), turned.astype(F32)
+            if both:
+                wt[rows] = (2.0 * tq - turned).astype(BF)
+            w[p, rows] = (2.0 * turned - tq).astype(BF)
+
+    def energy(p, read, first, second, slot):
         @pl.loop(0, 4)
         def _(q):
             rows = pl.ds(pl.multiple_of(128 * q, 128), 128)
             tq = read(q, slice(None)).astype(F32)
-            turned = jnp.concatenate([read(n, rows).T for n in range(4)], axis=1).astype(F32)
-            wide = 2.0 * tq - turned
             gap = vv[q] - eps[first, 0:1, :] - eps[second, 0:1, :]
+            wide = 2.0 * tq - tt[p, rows].astype(F32)
             esum[slot, 0:1] += jnp.sum(gap * tq * wide, axis=0, keepdims=True)
-            if both:
-                wt[rows] = wide.astype(BF)
-            w[rows] = (2.0 * turned - tq).astype(BF)
 
     def times(weight, factor):
-        return jnp.dot(weight[...], factor, preferred_element_type=F32)
-
-    arrive([to_far[3][2], ct_far[3]])
-
-    @even
-    def _():
-        to_far[3][3].wait_recv()
-        second_batch(2, sg, bx, 1, 3)
-
-    second_batch(0, sf, bo, 0, 2)
-    second_batch(1, sf, bx, 1, 2)
-
-    gram(acc, bo, bo, far, False)
-
-    @pl.loop(0, 4)
-    def _(q):
-        rows = pl.ds(pl.multiple_of(128 * q, 128), 128)
-        a0[q] = amplitude(acc[rows], 0, 0, q, slice(None))
-
-    pair(lambda q, cols: a0[q, :, cols], 0, 0, 0, False)
-    gown[...] = times(w, bo[g].reshape(512, 256))
+        return jnp.dot(weight, factor.reshape(512, 256), preferred_element_type=F32)
+
+    def amplitudes(p):
+        return lambda q, cols: t[p, q, :, cols]
+
+    def own_amplitudes(q, cols):
+        return a0[q, :, cols]
+
+    weights(3, own_amplitudes, False)
+    gown[...] = times(w[3], bo[g])
 
     @odd
     def _():
@@ -287,9 +319,9 @@
         def _(q):
             rows = pl.ds(pl.multiple_of(128 * q, 128), 128)
             t[2, q] = amplitude(acc2[rows], 1, 0, q, slice(None))
-        pair(lambda q, cols: t[2, q, :, cols], 1, 0, 3, True)
-        gown[...] += times(wt, bx[g].reshape(512, 256))
-        goth[...] = times(w, bo[g].reshape(512, 256))
+        weights(2, amplitudes(2), True)
+        gown[...] += times(wt[...], bx[g])
+        goth[...] = times(w[2], bo[g])
 
     c_f = copy(out3.at[0], in3.at[0], up1)
     c_g = copy(out3.at[1], in3.at[1], up2, "even")
@@ -298,23 +330,31 @@
     @even
     def _():
         arrive(early[2] + late[2])
-        pair(lambda q, cols: t[2, q, :, cols], 1, 3, 3, True)
-        out3[1] = times(wt, bx[g_up2].reshape(512, 256)).astype(BF)
+        weights(2, amplitudes(2), True)
+        out3[1] = times(wt[...], bx[g_up2]).astype(BF)
         c_g.start()
+
+    arrive(early[0] + late[0])
+    weights(0, amplitudes(0), True)
+    gf[...] = times(wt[...], bo[g_up1])
+    arrive(early[1] + late[1])
+    weights(1, amplitudes(1), True)
+    out3[0] = (gf[...] + times(wt[...], bx[g_up1])).astype(BF)
+    c_f.start()
+
+    @even
+    def _():
         cr_g.wait_recv()
-        goth[...] = times(w, rg[...].reshape(512, 256))
+        goth[...] = times(w[2], rg[...])
 
     cr_f.wait_recv()
-    arrive(early[0] + late[0])
-    pair(lambda q, cols: t[0, q, :, cols], 0, 2, 2, True)
-    gf[...] = times(wt, bo[g_up1].reshape(512, 256))
-    gown[...] += times(w, rf[...].reshape(512, 256))
-    arrive(early[1] + late[1])
-    pair(lambda q, cols: t[1, q, :, cols], 1, 2, 1, True)
-    out3[0] = (gf[...] + times(wt, bx[g_up1].reshape(512, 256))).astype(BF)
-    c_f.start()
-    out3[2] = (goth[...] + times(w, rf[...].reshape(512, 256))).astype(BF)
+    out3[2] = (goth[...] + times(w[1], rf[...])).astype(BF)
     c_x.start()
+    gown[...] += times(w[0], rf[...])
+    energy(3, own_amplitudes, 0, 0, 0)
+    energy(0, amplitudes(0), 0, 2, 2)
+    energy(1, amplitudes(1), 1, 2, 1)
+    energy(2, amplitudes(2), 1, 3 * (1 - k), 3)
 
     lane = lax.broadcasted_iota(jnp.int32, (8, 128), 1)
     total = [-jnp.sum(esum[n, 0:1], axis=1, keepdims=True) for n in range(4)]
@@ -372,8 +412,10 @@
             pltpu.VMEM((4, 128, 512), F32),
             pltpu.VMEM((512, 512), F32),
             pltpu.VMEM((512, 512), F32),
+            pltpu.VMEM((3, 4, 32, 512), F32),
+            pltpu.VMEM((4, 512, 512), BF),
             pltpu.VMEM((512, 512), BF),
-            pltpu.VMEM((512, 512), BF),
+            pltpu.VMEM((4, 512, 512), BF),
             pltpu.VMEM((512, 256), F32),
             pltpu.VMEM((512, 256), F32),
             pltpu.VMEM((512, 256), F32),

time: 86.6 us -> 91.2 us (1.053)
  Pallas kernels: 81.3 us -> 86 us
    pallas_call x1, Pallas kernels: 81.3 us -> 86 us  [per_device(): pl.pallas_call(kernel, out_shape=(jax.ShapeDtypeStruct((256, 512), F32),...]
where the time goes in v7:
time: 91.2 us; the launch traced here: 90.2 us
  Pallas kernels  86 us (94%)
  local copies, waits for them, and re-layouts  2.89 us (3%)
  between operations  1.29 us (1%)
    pallas_call x1, Pallas kernels, per_device(): pl.pallas_call(kernel, out_shape=(jax.ShapeDtypeStruct((256, 512), F32),...  86 us
    unnamed x4, local copies, waits for them, and re-layouts  2.89 us

profile of v7, /device:TPU:6, one launch (start us, length us, event | category | flops | bytes accessed | tf_op | source)
XLA Modules:
  0.0 90.2 jit_solution(3118095906391806450)
XLA Ops:
  1.3 86.0 %pairs.1 = (f32[256,512]{1,0:T(8,128)}, f32[1,4]{1,0:T(1,128)}) custom-call(bf16[256,512]{1,0:T(8,128)(2,1)} %bitcast.4, f32[1]{0:T(128)S(6)} %copy.7.occ_ref, f32[1,512]{1,0:T(1,128)} %bitcast.5), custom_call_target="tpu_custom_call" | custom-call | tf_op jit(solution)/shard_map/pairs/pallas_call | solution.py:394
  87.3 0.0 copy-start
  87.3 2.4 %copy.5 = f32[256,1,512]{2,1,0:T(1,128)} copy(f32[256,1,512]{2,0,1:T(8,128)} %bitcast.3) | data formatting | bytes 1048576
  89.7 0.0 copy-done
  89.7 0.5 copy.8
Async XLA Ops:
  87.3 2.4 %copy-start = (f32[1,4]{1,0:T(1,128)S(1)}, f32[1,4]{1,0:T(1,128)}, u32[]{:S(2)}) copy-start(f32[1,4]{1,0:T(1,128)} %get-tuple-element.10) | copy-start | bytes 52

commit v8 on v7

--- a/solution.py
+++ b/solution.py
@@ -11,7 +11,7 @@
 NX = 4
 NU = 64
 HALF = NU // 2
-COPIES = 128
+COPIES = 144
 
 
 def place(x, u, k):
@@ -146,14 +146,14 @@
         return first, second, f, g
 
     to_near = slices(near4, slice(None))
-    for n in range(2):
-        sent(cz[n])
-        cz[n + 2].start()
+    sent(cz[0])
+    cz[2].start()
     for c in cx:
         c.wait_recv()
     ct_near.start()
     to_near[0]()
-    sent(cz[2])
+    sent(cz[1])
+    cz[3].start()
     cz[4].start()
 
     def gram(dst, lhs, rhs, base, init):
@@ -212,7 +212,7 @@
             q = min(step, 4) - 1
             to_far[q][0]()
             ct_far[q].start()
-    for part in to_far:
+    for part in to_far[:3]:
         part[1]()
     pl.when(y == 0)(cr_f.start)
     pl.when((y < 2) & (k == 0))(cr_g.start)
@@ -221,36 +221,65 @@
         gap = vv[q, rows, cols] - eps[first, 0:1, cols] - eps[second, 0:1, cols]
         return (-integral / gap).astype(BF)
 
-    head, tail = slice(0, 384), slice(384, 512)
-    early = [[copy(t.at[p, 0:3, mine, head], t.at[p, 0:3, mine, head], xs[d], "even" if p == 2 else "all")
-              for d in range(3)] for p in range(3)]
-    late = [[copy(src, src, xs[d], "even" if p == 2 else "all") for d in range(3)
-             for src in (t.at[p, 3, mine], t.at[p, 0:3, mine, tail])] for p in range(3)]
-
-    def begin(copies):
-        for c in copies:
+    def parts(p, n):
+        if n == 1:
+            return [t.at[p, 0:2, mine, 0:256]]
+        upto, new = slice(0, 128 * n + 128), slice(128 * n, 128 * n + 128)
+        return [t.at[p, n, mine, upto], t.at[p, 0:n, mine, new]]
+
+    gather = [
+        [[copy(src, src, xs[d], "even" if p == 2 else "all") for d in range(3) for src in parts(p, n)] for n in (1, 2, 3)]
+        for p in range(3)
+    ]
+
+    def batch(p, n, piece, whole, base, first, second):
+        def block(rows, cols):
+            total = tile(piece, slice(*rows), whole, slice(*cols), base)
+            lanes = slice(128 * cols[0], 128 * cols[1])
+            for q in range(*rows):
+                start = 32 * (q - rows[0])
+                whole_sum = nacc[p, q, :, lanes] + total[start:start + 32]
+                t[p, q, mine, lanes] = amplitude(whole_sum, first, second, q, mine, lanes)
+
+        if n == 1:
+            block((0, 2), (0, 2))
+        else:
+            block((n, n + 1), (0, n + 1))
+            block((0, n), (n, n + 1))
+        for c in gather[p][n - 1]:
             c.start()
 
-    def first_batch(p, piece, whole, base, first, second):
-        total = tile(piece, slice(0, 3), whole, slice(0, 3), base)
-        for q in range(3):
-            whole_sum = nacc[p, q, :, head] + total[32 * q:32 * q + 32]
-            t[p, q, mine, head] = amplitude(whole_sum, first, second, q, mine, head)
-        begin(early[p])
-
-    def second_batch(p, piece, whole, base, first, second):
-        total = nacc[p, 3] + tile(piece, slice(3, 4), whole, every, base)
-        t[p, 3, mine] = amplitude(total, first, second, 3, mine)
-        total = tile(piece, slice(0, 3), whole, slice(3, 4), base)
-        for q in range(3):
-            whole_sum = nacc[p, q, :, tail] + total[32 * q:32 * q + 32]
-            t[p, q, mine, tail] = amplitude(whole_sum, first, second, q, mine, tail)
-        begin(late[p])
-
-    @even
-    def _():
-        to_near[3].wait_recv()
-        pl.when(h_up2 == h)(lambda: half(2, sg, bx, first_2))
+    def next_chip(n):
+        batch(0, n, sf, bo, last_1, 0, 2)
+        batch(1, n, sf, bx, last_1, 1, 2)
+
+    def chip_after(n):
+        batch(2, n, sg, bx, last_2, 1, 3)
+
+    arrive(ce + [part[2] for part in to_far[:2]] + ct_far[:2])
+
+    @pl.when(h_up1 != h)
+    def _():
+        arrive(ct_far[2:])
+        halves()
+
+    next_chip(1)
+    pl.when(h_up1 == h)(lambda: arrive(ct_far[2:]))
+    to_far[3][1]()
+
+    @even
+    def _():
+        arrive([to_near[3]] + [part[3] for part in to_far[:2]])
+        half(2, sg, bx, first_2)
+        chip_after(1)
+
+    to_far[2][2].wait_recv()
+    next_chip(2)
+
+    @even
+    def _():
+        to_far[2][3].wait_recv()
+        chip_after(2)
 
     gram(acc, bo, bo, far, False)
 
@@ -259,25 +288,13 @@
         rows = pl.ds(pl.multiple_of(128 * q, 128), 128)
         a0[q] = amplitude(acc[rows], 0, 0, q, slice(None))
 
-    arrive(ce + [part[2] for part in to_far[:3]] + ct_far)
-    pl.when(h_up1 != h)(halves)
-    first_batch(0, sf, bo, last_1, 0, 2)
-    first_batch(1, sf, bx, last_1, 1, 2)
-
-    @even
-    def _():
-        arrive([part[3] for part in to_far[:3]])
-        pl.when(h_up2 != h)(lambda: half(2, sg, bx, first_2))
-        first_batch(2, sg, bx, last_2, 1, 3)
-
     to_far[3][2].wait_recv()
-    second_batch(0, sf, bo, last_1, 0, 2)
-    second_batch(1, sf, bx, last_1, 1, 2)
+    next_chip(3)
 
     @even
     def _():
         to_far[3][3].wait_recv()
-        second_batch(2, sg, bx, last_2, 1, 3)
+        chip_after(3)
 
     def weights(p, read, both):
         @pl.loop(0, 4)
@@ -329,15 +346,15 @@
 
     @even
     def _():
-        arrive(early[2] + late[2])
+        arrive(sum(gather[2], []))
         weights(2, amplitudes(2), True)
         out3[1] = times(wt[...], bx[g_up2]).astype(BF)
         c_g.start()
 
-    arrive(early[0] + late[0])
+    arrive(sum(gather[0], []))
     weights(0, amplitudes(0), True)
     gf[...] = times(wt[...], bo[g_up1])
-    arrive(early[1] + late[1])
+    arrive(sum(gather[1], []))
     weights(1, amplitudes(1), True)
     out3[0] = (gf[...] + times(wt[...], bx[g_up1])).astype(BF)
     c_f.start()

time: 91.2 us -> 87.5 us (0.959)
  Pallas kernels: 86 us -> 82.7 us
    pallas_call x1, Pallas kernels: 86 us -> 82.7 us  [per_device(): pl.pallas_call(kernel, out_shape=(jax.ShapeDtypeStruct((256, 512), F32),...]
where the time goes in v8:
time: 87.5 us; the launch traced here: 86.9 us
  Pallas kernels  82.7 us (95%)
  local copies, waits for them, and re-layouts  2.89 us (3%)
  between operations  1.29 us (1%)
    pallas_call x1, Pallas kernels, per_device(): pl.pallas_call(kernel, out_shape=(jax.ShapeDtypeStruct((256, 512), F32),...  82.7 us
    unnamed x4, local copies, waits for them, and re-layouts  2.89 us

profile of v8, /device:TPU:6, one launch (start us, length us, event | category | flops | bytes accessed | tf_op | source)
XLA Modules:
  0.0 86.9 jit_solution(4506077162891814116)
XLA Ops:
  1.3 82.7 %pairs.1 = (f32[256,512]{1,0:T(8,128)}, f32[1,4]{1,0:T(1,128)}) custom-call(bf16[256,512]{1,0:T(8,128)(2,1)} %bitcast.4, f32[1]{0:T(128)S(6)} %copy.7.occ_ref, f32[1,512]{1,0:T(1,128)} %bitcast.5), custom_call_target="tpu_custom_call" | custom-call | tf_op jit(solution)/shard_map/pairs/pallas_call | solution.py:411
  84.0 0.0 copy-start
  84.0 2.4 %copy.5 = f32[256,1,512]{2,1,0:T(1,128)} copy(f32[256,1,512]{2,0,1:T(8,128)} %bitcast.3) | data formatting | bytes 1048576
  86.4 0.0 copy-done
  86.4 0.5 copy.8
Async XLA Ops:
  84.0 2.4 %copy-start = (f32[1,4]{1,0:T(1,128)S(1)}, f32[1,4]{1,0:T(1,128)}, u32[]{:S(2)}) copy-start(f32[1,4]{1,0:T(1,128)} %get-tuple-element.10) | copy-start | bytes 52

commit v9 on v8

--- a/solution.py
+++ b/solution.py
@@ -221,16 +221,34 @@
         gap = vv[q, rows, cols] - eps[first, 0:1, cols] - eps[second, 0:1, cols]
         return (-integral / gap).astype(BF)
 
-    def parts(p, n):
+    def parts(p, n, rows):
         if n == 1:
-            return [t.at[p, 0:2, mine, 0:256]]
+            return [t.at[p, 0:2, rows, 0:256]]
         upto, new = slice(0, 128 * n + 128), slice(128 * n, 128 * n + 128)
-        return [t.at[p, n, mine, upto], t.at[p, 0:n, mine, new]]
-
-    gather = [
-        [[copy(src, src, xs[d], "even" if p == 2 else "all") for d in range(3) for src in parts(p, n)] for n in (1, 2, 3)]
-        for p in range(3)
+        return [t.at[p, n, rows, upto], t.at[p, 0:n, rows, new]]
+
+    step_x = 1 - 2 * k
+    ahead, behind = place(x + NX + step_x, u, k), place(x + NX - step_x, u, k)
+    theirs = pl.ds(pl.multiple_of(32 * lax.rem(x + NX - step_x, NX), 32), 32)
+    by_core = ["all", "all", "even"]
+    to_ahead, to_behind, passed = [
+        [[[copy(src, src, device, by_core[p]) for src in parts(p, n, rows)] for n in (1, 2, 3)] for p in range(3)]
+        for device, rows in ((ahead, mine), (behind, mine), (ahead, theirs))
     ]
+
+    def pass_on(p, n):
+        for got, on in zip(to_ahead[p][n - 1], passed[p][n - 1]):
+            got.wait_recv()
+            on.start()
+
+    def pass_all(n):
+        pass_on(0, n)
+        pass_on(1, n)
+        even(lambda: pass_on(2, n))
+
+    def gathered(p):
+        for n in range(3):
+            arrive(to_behind[p][n] + passed[p][n])
 
     def batch(p, n, piece, whole, base, first, second):
         def block(rows, cols):
@@ -246,7 +264,7 @@
         else:
             block((n, n + 1), (0, n + 1))
             block((0, n), (n, n + 1))
-        for c in gather[p][n - 1]:
+        for c in to_ahead[p][n - 1] + to_behind[p][n - 1]:
             c.start()
 
     def next_chip(n):
@@ -280,6 +298,8 @@
     def _():
         to_far[2][3].wait_recv()
         chip_after(2)
+
+    pass_all(1)
 
     gram(acc, bo, bo, far, False)
 
@@ -295,6 +315,8 @@
     def _():
         to_far[3][3].wait_recv()
         chip_after(3)
+
+    pass_all(2)
 
     def weights(p, read, both):
         @pl.loop(0, 4)
@@ -328,6 +350,8 @@
     weights(3, own_amplitudes, False)
     gown[...] = times(w[3], bo[g])
 
+    pass_all(3)
+
     @odd
     def _():
         gram(acc2, bo, bx, far, False)
@@ -341,22 +365,29 @@
         goth[...] = times(w[2], bo[g])
 
     c_f = copy(out3.at[0], in3.at[0], up1)
-    c_g = copy(out3.at[1], in3.at[1], up2, "even")
+    c_g = copy(out3.at[1], in3.at[1], up1, "even")
     c_x = copy(out3.at[2], in3.at[2], twin)
 
     @even
     def _():
-        arrive(sum(gather[2], []))
+        gathered(2)
         weights(2, amplitudes(2), True)
         out3[1] = times(wt[...], bx[g_up2]).astype(BF)
         c_g.start()
 
-    arrive(sum(gather[0], []))
+    gathered(0)
     weights(0, amplitudes(0), True)
     gf[...] = times(wt[...], bo[g_up1])
-    arrive(sum(gather[1], []))
+    gathered(1)
     weights(1, amplitudes(1), True)
-    out3[0] = (gf[...] + times(wt[...], bx[g_up1])).astype(BF)
+    gf[...] += times(wt[...], bx[g_up1])
+
+    @even
+    def _():
+        c_g.wait_recv()
+        gf[...] += in3[1].astype(F32)
+
+    out3[0] = gf[...].astype(BF)
     c_f.start()
 
     @even
@@ -387,11 +418,6 @@
     gown[...] += in3[2].astype(F32)
     c_f.wait_recv()
     gown[...] += in3[0].astype(F32)
-
-    @even
-    def _():
-        c_g.wait_recv()
-        gown[...] += in3[1].astype(F32)
 
     for n in range(4):
         gamma_ref[:, 128 * n:128 * n + 128] = gown[128 * n:128 * n + 128].T

time: 87.5 us -> 91.8 us (1.049)
  Pallas kernels: 82.7 us -> 86.8 us
    pallas_call x1, Pallas kernels: 82.7 us -> 86.8 us  [per_device(): pl.pallas_call(kernel, out_shape=(jax.ShapeDtypeStruct((256, 512), F32),...]
where the time goes in v9:
time: 91.8 us; the launch traced here: 91 us
  Pallas kernels  86.8 us (95%)
  local copies, waits for them, and re-layouts  2.89 us (3%)
  between operations  1.29 us (1%)
    pallas_call x1, Pallas kernels, per_device(): pl.pallas_call(kernel, out_shape=(jax.ShapeDtypeStruct((256, 512), F32),...  86.8 us
    unnamed x4, local copies, waits for them, and re-layouts  2.89 us

profile of v9, /device:TPU:6, one launch (start us, length us, event | category | flops | bytes accessed | tf_op | source)
XLA Modules:
  0.0 91.0 jit_solution(9457676512523216040)
XLA Ops:
  1.3 86.8 %pairs.1 = (f32[256,512]{1,0:T(8,128)}, f32[1,4]{1,0:T(1,128)}) custom-call(bf16[256,512]{1,0:T(8,128)(2,1)} %bitcast.4, f32[1]{0:T(128)S(6)} %copy.7.occ_ref, f32[1,512]{1,0:T(1,128)} %bitcast.5), custom_call_target="tpu_custom_call" | custom-call | tf_op jit(solution)/shard_map/pairs/pallas_call | solution.py:437
  88.1 0.0 copy-start
  88.1 2.4 %copy.5 = f32[256,1,512]{2,1,0:T(1,128)} copy(f32[256,1,512]{2,0,1:T(8,128)} %bitcast.3) | data formatting | bytes 1048576
  90.5 0.0 copy-done
  90.5 0.5 copy.8
Async XLA Ops:
  88.1 2.4 %copy-start = (f32[1,4]{1,0:T(1,128)S(1)}, f32[1,4]{1,0:T(1,128)}, u32[]{:S(2)}) copy-start(f32[1,4]{1,0:T(1,128)} %get-tuple-element.10) | copy-start | bytes 52

commit v10 on v8

--- a/solution.py
+++ b/solution.py
@@ -341,7 +341,7 @@
         goth[...] = times(w[2], bo[g])
 
     c_f = copy(out3.at[0], in3.at[0], up1)
-    c_g = copy(out3.at[1], in3.at[1], up2, "even")
+    c_g = copy(out3.at[1], in3.at[1], up1, "even")
     c_x = copy(out3.at[2], in3.at[2], twin)
 
     @even
@@ -356,7 +356,14 @@
     gf[...] = times(wt[...], bo[g_up1])
     arrive(sum(gather[1], []))
     weights(1, amplitudes(1), True)
-    out3[0] = (gf[...] + times(wt[...], bx[g_up1])).astype(BF)
+    gf[...] += times(wt[...], bx[g_up1])
+
+    @even
+    def _():
+        c_g.wait_recv()
+        gf[...] += in3[1].astype(F32)
+
+    out3[0] = gf[...].astype(BF)
     c_f.start()
 
     @even
@@ -387,11 +394,6 @@
     gown[...] += in3[2].astype(F32)
     c_f.wait_recv()
     gown[...] += in3[0].astype(F32)
-
-    @even
-    def _():
-        c_g.wait_recv()
-        gown[...] += in3[1].astype(F32)
 
     for n in range(4):
         gamma_ref[:, 128 * n:128 * n + 128] = gown[128 * n:128 * n + 128].T

time: 87.5 us -> 89.6 us (1.024)
  Pallas kernels: 82.7 us -> 84.7 us
    pallas_call x1, Pallas kernels: 82.7 us -> 84.7 us  [per_device(): pl.pallas_call(kernel, out_shape=(jax.ShapeDtypeStruct((256, 512), F32),...]
where the time goes in v10:
time: 89.6 us; the launch traced here: 88.9 us
  Pallas kernels  84.7 us (95%)
  local copies, waits for them, and re-layouts  2.89 us (3%)
  between operations  1.29 us (1%)
    pallas_call x1, Pallas kernels, per_device(): pl.pallas_call(kernel, out_shape=(jax.ShapeDtypeStruct((256, 512), F32),...  84.7 us
    unnamed x4, local copies, waits for them, and re-layouts  2.89 us

profile of v10, /device:TPU:6, one launch (start us, length us, event | category | flops | bytes accessed | tf_op | source)
XLA Modules:
  0.0 88.9 jit_solution(7931283975500448162)
XLA Ops:
  1.3 84.7 %pairs.1 = (f32[256,512]{1,0:T(8,128)}, f32[1,4]{1,0:T(1,128)}) custom-call(bf16[256,512]{1,0:T(8,128)(2,1)} %bitcast.4, f32[1]{0:T(128)S(6)} %copy.7.occ_ref, f32[1,512]{1,0:T(1,128)} %bitcast.5), custom_call_target="tpu_custom_call" | custom-call | tf_op jit(solution)/shard_map/pairs/pallas_call | solution.py:413
  86.0 0.0 copy-start
  86.0 2.4 %copy.5 = f32[256,1,512]{2,1,0:T(1,128)} copy(f32[256,1,512]{2,0,1:T(8,128)} %bitcast.3) | data formatting | bytes 1048576
  88.3 0.0 copy-done
  88.3 0.5 copy.8
Async XLA Ops:
  86.0 2.4 %copy-start = (f32[1,4]{1,0:T(1,128)S(1)}, f32[1,4]{1,0:T(1,128)}, u32[]{:S(2)}) copy-start(f32[1,4]{1,0:T(1,128)} %get-tuple-element.10) | copy-start | bytes 52

commit v11 on v8

--- a/solution.py
+++ b/solution.py
@@ -288,14 +288,6 @@
         rows = pl.ds(pl.multiple_of(128 * q, 128), 128)
         a0[q] = amplitude(acc[rows], 0, 0, q, slice(None))
 
-    to_far[3][2].wait_recv()
-    next_chip(3)
-
-    @even
-    def _():
-        to_far[3][3].wait_recv()
-        chip_after(3)
-
     def weights(p, read, both):
         @pl.loop(0, 4)
         def _(q):
@@ -325,11 +317,11 @@
     def own_amplitudes(q, cols):
         return a0[q, :, cols]
 
-    weights(3, own_amplitudes, False)
-    gown[...] = times(w[3], bo[g])
-
-    @odd
-    def _():
+    def own_pair():
+        weights(3, own_amplitudes, False)
+        gown[...] = times(w[3], bo[g])
+
+    def chip_pair():
         gram(acc2, bo, bx, far, False)
 
         @pl.loop(0, 4)
@@ -339,6 +331,20 @@
         weights(2, amplitudes(2), True)
         gown[...] += times(wt[...], bx[g])
         goth[...] = times(w[2], bo[g])
+
+    @odd
+    def _():
+        own_pair()
+        chip_pair()
+
+    @even
+    def _():
+        to_far[3][3].wait_recv()
+        chip_after(3)
+
+    to_far[3][2].wait_recv()
+    next_chip(3)
+    even(own_pair)
 
     c_f = copy(out3.at[0], in3.at[0], up1)
     c_g = copy(out3.at[1], in3.at[1], up2, "even")

time: 87.5 us -> 86.5 us (0.989)
  Pallas kernels: 82.7 us -> 81.5 us
    pallas_call x1, Pallas kernels: 82.7 us -> 81.5 us  [per_device(): pl.pallas_call(kernel, out_shape=(jax.ShapeDtypeStruct((256, 512), F32),...]
where the time goes in v11:
time: 86.5 us; the launch traced here: 85.7 us
  Pallas kernels  81.5 us (94%)
  local copies, waits for them, and re-layouts  2.89 us (3%)
  between operations  1.29 us (1%)
    pallas_call x1, Pallas kernels, per_device(): pl.pallas_call(kernel, out_shape=(jax.ShapeDtypeStruct((256, 512), F32),...  81.5 us
    unnamed x4, local copies, waits for them, and re-layouts  2.89 us

profile of v11, /device:TPU:6, one launch (start us, length us, event | category | flops | bytes accessed | tf_op | source)
XLA Modules:
  0.0 85.7 jit_solution(2145073726637517460)
XLA Ops:
  1.3 81.5 %pairs.1 = (f32[256,512]{1,0:T(8,128)}, f32[1,4]{1,0:T(1,128)}) custom-call(bf16[256,512]{1,0:T(8,128)(2,1)} %bitcast.4, f32[1]{0:T(128)S(6)} %copy.7.occ_ref, f32[1,512]{1,0:T(1,128)} %bitcast.5), custom_call_target="tpu_custom_call" | custom-call | tf_op jit(solution)/shard_map/pairs/pallas_call | solution.py:417
  82.8 0.0 copy-start
  82.8 2.4 %copy.5 = f32[256,1,512]{2,1,0:T(1,128)} copy(f32[256,1,512]{2,0,1:T(8,128)} %bitcast.3) | data formatting | bytes 1048576
  85.2 0.0 copy-done
  85.2 0.5 copy.8
Async XLA Ops:
  82.8 2.4 %copy-start = (f32[1,4]{1,0:T(1,128)S(1)}, f32[1,4]{1,0:T(1,128)}, u32[]{:S(2)}) copy-start(f32[1,4]{1,0:T(1,128)} %get-tuple-element.10) | copy-start | bytes 52

commit v12 on v11

--- a/solution.py
+++ b/solution.py
@@ -26,7 +26,7 @@
 def kernel(
     f_ref, occ_ref, vir_ref, gamma_ref, energy_ref,
     bo, bx, sf, sg, sv, rf, rg, t, a0, vv, acc, acc2, nacc, w, wt, tt,
-    gown, goth, gf, out3, in3, eps, esum, en, f_own, vir, local, send, recv,
+    gown, goth, gf, out3, in3, between, eps, esum, en, f_own, vir, local, send, recv,
 ):
     b = lax.axis_index("blk")
     a = lax.axis_index("aux")
@@ -52,7 +52,10 @@
 
     barrier = pltpu.get_barrier_semaphore()
     down4, up4 = place(x, u + NU - 4, k), place(x, u + 4, k)
-    others = xs + [partner, twin, down1, down2, up1, up2, down4, up4]
+    down3, up3 = place(x, u + NU - 3, k), place(x, u + 3, k)
+    way_back = place(x, u + NU - 1 + 4 * lax.div(3 - y, 3), k)
+    passed_to = place(x, u + NU + 3 - 4 * lax.div(y, 3), k)
+    others = xs + [partner, twin, down1, down2, up1, up2, down4, up4, down3, up3]
     for device in others:
         pl.semaphore_signal(barrier, inc=1, device_id=device, device_id_type=MESH)
 
@@ -347,7 +350,8 @@
     even(own_pair)
 
     c_f = copy(out3.at[0], in3.at[0], up1)
-    c_g = copy(out3.at[1], in3.at[1], up2, "even")
+    c_g = copy(out3.at[1], between, way_back, "even")
+    c_g_on = copy(between, in3.at[1], passed_to, "even")
     c_x = copy(out3.at[2], in3.at[2], twin)
 
     @even
@@ -373,6 +377,12 @@
     cr_f.wait_recv()
     out3[2] = (goth[...] + times(w[1], rf[...])).astype(BF)
     c_x.start()
+
+    @even
+    def _():
+        c_g.wait_recv()
+        c_g_on.start()
+
     gown[...] += times(w[0], rf[...])
     energy(3, own_amplitudes, 0, 0, 0)
     energy(0, amplitudes(0), 0, 2, 2)
@@ -396,7 +406,7 @@
 
     @even
     def _():
-        c_g.wait_recv()
+        c_g_on.wait_recv()
         gown[...] += in3[1].astype(F32)
 
     for n in range(4):
@@ -444,6 +454,7 @@
             pltpu.VMEM((512, 256), F32),
             pltpu.VMEM((3, 512, 256), BF),
             pltpu.VMEM((3, 512, 256), BF),
+            pltpu.VMEM((512, 256), BF),
             pltpu.VMEM((4, 8, 512), F32),
             pltpu.VMEM((4, 8, 512), F32),
             pltpu.VMEM((2, 8, 128), F32),

time: 86.5 us -> 87.9 us (1.016)
  Pallas kernels: 81.5 us -> 82.4 us
where the time goes in v12:
time: 87.9 us; the launch traced here: 86.6 us
  Pallas kernels  82.4 us (94%)
  local copies, waits for them, and re-layouts  2.89 us (3%)
  between operations  1.29 us (1%)
    pallas_call x1, Pallas kernels, per_device(): pl.pallas_call(kernel, out_shape=(jax.ShapeDtypeStruct((256, 512), F32),...  82.4 us
    unnamed x4, local copies, waits for them, and re-layouts  2.89 us

profile of v12, /device:TPU:6, one launch (start us, length us, event | category | flops | bytes accessed | tf_op | source)
XLA Modules:
  0.0 86.6 jit_solution(16906086258915458843)
XLA Ops:
  1.3 82.4 %pairs.1 = (f32[256,512]{1,0:T(8,128)}, f32[1,4]{1,0:T(1,128)}) custom-call(bf16[256,512]{1,0:T(8,128)(2,1)} %bitcast.4, f32[1]{0:T(128)S(6)} %copy.7.occ_ref, f32[1,512]{1,0:T(1,128)} %bitcast.5), custom_call_target="tpu_custom_call" | custom-call | tf_op jit(solution)/shard_map/pairs/pallas_call | solution.py:427
  83.7 0.0 copy-start
  83.7 2.4 %copy.5 = f32[256,1,512]{2,1,0:T(1,128)} copy(f32[256,1,512]{2,0,1:T(8,128)} %bitcast.3) | data formatting | bytes 1048576
  86.1 0.0 copy-done
  86.1 0.5 copy.8
Async XLA Ops:
  83.7 2.4 %copy-start = (f32[1,4]{1,0:T(1,128)S(1)}, f32[1,4]{1,0:T(1,128)}, u32[]{:S(2)}) copy-start(f32[1,4]{1,0:T(1,128)} %get-tuple-element.10) | copy-start | bytes 52

commit v13 on v11

--- a/solution.py
+++ b/solution.py
@@ -214,8 +214,6 @@
             ct_far[q].start()
     for part in to_far[:3]:
         part[1]()
-    pl.when(y == 0)(cr_f.start)
-    pl.when((y < 2) & (k == 0))(cr_g.start)
 
     def amplitude(integral, first, second, q, rows, cols=slice(None)):
         gap = vv[q, rows, cols] - eps[first, 0:1, cols] - eps[second, 0:1, cols]
@@ -344,6 +342,8 @@
 
     to_far[3][2].wait_recv()
     next_chip(3)
+    pl.when(y == 0)(cr_f.start)
+    pl.when((y < 2) & (k == 0))(cr_g.start)
     even(own_pair)
 
     c_f = copy(out3.at[0], in3.at[0], up1)

time: 86.5 us -> 87.4 us (1.010)
  the two profiles are of different devices: /device:TPU:6 before, /device:TPU:17 now
where the time goes in v13:
time: 87.4 us; the launch traced here: 87.3 us
  Pallas kernels  83.1 us (95%)
  local copies, waits for them, and re-layouts  2.89 us (3%)
  between operations  1.29 us (1%)
    pallas_call x1, Pallas kernels, per_device(): pl.pallas_call(kernel, out_shape=(jax.ShapeDtypeStruct((256, 512), F32),...  83.1 us
    unnamed x4, local copies, waits for them, and re-layouts  2.89 us

profile of v13, /device:TPU:17, one launch (start us, length us, event | category | flops | bytes accessed | tf_op | source)
XLA Modules:
  0.0 87.3 jit_solution(4522176185261755428)
XLA Ops:
  1.3 83.1 %pairs.1 = (f32[256,512]{1,0:T(8,128)}, f32[1,4]{1,0:T(1,128)}) custom-call(bf16[256,512]{1,0:T(8,128)(2,1)} %bitcast.4, f32[1]{0:T(128)S(6)} %copy.7.occ_ref, f32[1,512]{1,0:T(1,128)} %bitcast.5), custom_call_target="tpu_custom_call" | custom-call | tf_op jit(solution)/shard_map/pairs/pallas_call | solution.py:417
  84.4 0.0 copy-start
  84.4 2.4 %copy.5 = f32[256,1,512]{2,1,0:T(1,128)} copy(f32[256,1,512]{2,0,1:T(8,128)} %bitcast.3) | data formatting | bytes 1048576
  86.8 0.0 copy-done
  86.8 0.5 copy.8
Async XLA Ops:
  84.4 2.4 %copy-start = (f32[1,4]{1,0:T(1,128)S(1)}, f32[1,4]{1,0:T(1,128)}, u32[]{:S(2)}) copy-start(f32[1,4]{1,0:T(1,128)} %get-tuple-element.10) | copy-start | bytes 52

commit v14 on v11

--- a/solution.py
+++ b/solution.py
@@ -337,25 +337,18 @@
         own_pair()
         chip_pair()
 
+    to_far[3][2].wait_recv()
+    next_chip(3)
+
     @even
     def _():
         to_far[3][3].wait_recv()
         chip_after(3)
-
-    to_far[3][2].wait_recv()
-    next_chip(3)
-    even(own_pair)
+        own_pair()
 
     c_f = copy(out3.at[0], in3.at[0], up1)
     c_g = copy(out3.at[1], in3.at[1], up2, "even")
     c_x = copy(out3.at[2], in3.at[2], twin)
-
-    @even
-    def _():
-        arrive(sum(gather[2], []))
-        weights(2, amplitudes(2), True)
-        out3[1] = times(wt[...], bx[g_up2]).astype(BF)
-        c_g.start()
 
     arrive(sum(gather[0], []))
     weights(0, amplitudes(0), True)
@@ -367,6 +360,10 @@
 
     @even
     def _():
+        arrive(sum(gather[2], []))
+        weights(2, amplitudes(2), True)
+        out3[1] = times(wt[...], bx[g_up2]).astype(BF)
+        c_g.start()
         cr_g.wait_recv()
         goth[...] = times(w[2], rg[...])
 

time: 86.5 us -> 87.7 us (1.014)
  the two profiles are of different devices: /device:TPU:6 before, /device:TPU:48 now
where the time goes in v14:
time: 87.7 us; the launch traced here: 87.6 us
  Pallas kernels  83.4 us (95%)
  local copies, waits for them, and re-layouts  2.89 us (3%)
  between operations  1.29 us (1%)
    pallas_call x1, Pallas kernels, per_device(): pl.pallas_call(kernel, out_shape=(jax.ShapeDtypeStruct((256, 512), F32),...  83.4 us
    unnamed x4, local copies, waits for them, and re-layouts  2.89 us

profile of v14, /device:TPU:48, one launch (start us, length us, event | category | flops | bytes accessed | tf_op | source)
XLA Modules:
  0.0 87.6 jit_solution(10726025912780194900)
XLA Ops:
  1.3 83.4 %pairs.1 = (f32[256,512]{1,0:T(8,128)}, f32[1,4]{1,0:T(1,128)}) custom-call(bf16[256,512]{1,0:T(8,128)(2,1)} %bitcast.4, f32[1]{0:T(128)S(6)} %copy.7.occ_ref, f32[1,512]{1,0:T(1,128)} %bitcast.5), custom_call_target="tpu_custom_call" | custom-call | tf_op jit(solution)/shard_map/pairs/pallas_call | solution.py:414
  84.7 0.0 copy-start
  84.7 2.4 %copy.5 = f32[256,1,512]{2,1,0:T(1,128)} copy(f32[256,1,512]{2,0,1:T(8,128)} %bitcast.3) | data formatting | bytes 1048576
  87.1 0.0 copy-done
  87.1 0.5 copy.8
Async XLA Ops:
  84.7 2.4 %copy-start = (f32[1,4]{1,0:T(1,128)S(1)}, f32[1,4]{1,0:T(1,128)}, u32[]{:S(2)}) copy-start(f32[1,4]{1,0:T(1,128)} %get-tuple-element.10) | copy-start | bytes 52

commit v15 on v11

--- a/solution.py
+++ b/solution.py
@@ -228,7 +228,7 @@
         return [t.at[p, n, mine, upto], t.at[p, 0:n, mine, new]]
 
     gather = [
-        [[copy(src, src, xs[d], "even" if p == 2 else "all") for d in range(3) for src in parts(p, n)] for n in (1, 2, 3)]
+        [[copy(src, src, xs[d], "even" if p == 2 else "all") for d in (1, 0, 2) for src in parts(p, n)] for n in (1, 2, 3)]
         for p in range(3)
     ]
 
@@ -273,13 +273,13 @@
         half(2, sg, bx, first_2)
         chip_after(1)
 
+    @even
+    def _():
+        to_far[2][3].wait_recv()
+        chip_after(2)
+
     to_far[2][2].wait_recv()
     next_chip(2)
-
-    @even
-    def _():
-        to_far[2][3].wait_recv()
-        chip_after(2)
 
     gram(acc, bo, bo, far, False)
 

time: 86.5 us -> 87.3 us (level)
  no operation moved by 1% of the time
where the time goes in v15:
time: 87.3 us; the launch traced here: 85.7 us
  Pallas kernels  81.5 us (93%)
  local copies, waits for them, and re-layouts  2.89 us (3%)
  between operations  1.29 us (1%)
    pallas_call x1, Pallas kernels, per_device(): pl.pallas_call(kernel, out_shape=(jax.ShapeDtypeStruct((256, 512), F32),...  81.5 us
    unnamed x4, local copies, waits for them, and re-layouts  2.89 us

profile of v15, /device:TPU:6, one launch (start us, length us, event | category | flops | bytes accessed | tf_op | source)
XLA Modules:
  0.0 85.7 jit_solution(16608700065541859976)
XLA Ops:
  1.3 81.5 %pairs.1 = (f32[256,512]{1,0:T(8,128)}, f32[1,4]{1,0:T(1,128)}) custom-call(bf16[256,512]{1,0:T(8,128)(2,1)} %bitcast.4, f32[1]{0:T(128)S(6)} %copy.7.occ_ref, f32[1,512]{1,0:T(1,128)} %bitcast.5), custom_call_target="tpu_custom_call" | custom-call | tf_op jit(solution)/shard_map/pairs/pallas_call | solution.py:417
  82.8 0.0 copy-start
  82.8 2.4 %copy.5 = f32[256,1,512]{2,1,0:T(1,128)} copy(f32[256,1,512]{2,0,1:T(8,128)} %bitcast.3) | data formatting | bytes 1048576
  85.2 0.0 copy-done
  85.2 0.5 copy.8
Async XLA Ops:
  82.8 2.4 %copy-start = (f32[1,4]{1,0:T(1,128)S(1)}, f32[1,4]{1,0:T(1,128)}, u32[]{:S(2)}) copy-start(f32[1,4]{1,0:T(1,128)} %get-tuple-element.10) | copy-start | bytes 52

commit v16 on v6

--- a/solution.py
+++ b/solution.py
@@ -25,7 +25,7 @@
 
 def kernel(
     f_ref, occ_ref, vir_ref, gamma_ref, energy_ref,
-    bo, bx, sf, sg, sv, rf, rg, t, a0, vv, acc, acc2, w, wt,
+    bo, bx, sf, sg, sv, rf, rg, t, a0, vv, acc, acc2, w, wt, tt,
     gown, goth, gf, out3, in3, eps, esum, en, f_own, vir, local, send, recv,
 ):
     b = lax.axis_index("blk")
@@ -243,21 +243,49 @@
         arrive([to_near[3]] + [part[3] for part in to_far[:3]])
         first_batch(2, sg, bx, 1, 3)
 
-    def pair(read, first, second, slot, both):
+    def weights(p, read, both):
+        @pl.loop(0, 4)
+        def _(q):
+            rows = pl.ds(pl.multiple_of(128 * q, 128), 128)
+            turned = jnp.concatenate([read(n, rows).T for n in range(4)], axis=1)
+            tt[p, rows] = turned
+            tq, turned = read(q, slice(None)).astype(F32), turned.astype(F32)
+            if both:
+                wt[rows] = (2.0 * tq - turned).astype(BF)
+            w[p, rows] = (2.0 * turned - tq).astype(BF)
+
+    def energy(p, read, first, second, slot):
         @pl.loop(0, 4)
         def _(q):
             rows = pl.ds(pl.multiple_of(128 * q, 128), 128)
             tq = read(q, slice(None)).astype(F32)
-            turned = jnp.concatenate([read(n, rows).T for n in range(4)], axis=1).astype(F32)
-            wide = 2.0 * tq - turned
             gap = vv[q] - eps[first, 0:1, :] - eps[second, 0:1, :]
+            wide = 2.0 * tq - tt[p, rows].astype(F32)
             esum[slot, 0:1] += jnp.sum(gap * tq * wide, axis=0, keepdims=True)
-            if both:
-                wt[rows] = wide.astype(BF)
-            w[rows] = (2.0 * turned - tq).astype(BF)
 
     def times(weight, factor):
-        return jnp.dot(weight[...], factor, preferred_element_type=F32)
+        return jnp.dot(weight, factor.reshape(512, 256), preferred_element_type=F32)
+
+    def amplitudes(p):
+        return lambda q, cols: t[p, q, :, cols]
+
+    def own_amplitudes(q, cols):
+        return a0[q, :, cols]
+
+    def own_pair():
+        weights(3, own_amplitudes, False)
+        gown[...] = times(w[3], bo[g])
+
+    def chip_pair():
+        gram(acc2, bo, bx, far, False)
+
+        @pl.loop(0, 4)
+        def _(q):
+            rows = pl.ds(pl.multiple_of(128 * q, 128), 128)
+            t[2, q] = amplitude(acc2[rows], 1, 0, q, slice(None))
+        weights(2, amplitudes(2), True)
+        gown[...] += times(wt[...], bx[g])
+        goth[...] = times(w[2], bo[g])
 
     arrive([to_far[3][2], ct_far[3]])
 
@@ -276,20 +304,8 @@
         rows = pl.ds(pl.multiple_of(128 * q, 128), 128)
         a0[q] = amplitude(acc[rows], 0, 0, q, slice(None))
 
-    pair(lambda q, cols: a0[q, :, cols], 0, 0, 0, False)
-    gown[...] = times(w, bo[g].reshape(512, 256))
-
-    @odd
-    def _():
-        gram(acc2, bo, bx, far, False)
-
-        @pl.loop(0, 4)
-        def _(q):
-            rows = pl.ds(pl.multiple_of(128 * q, 128), 128)
-            t[2, q] = amplitude(acc2[rows], 1, 0, q, slice(None))
-        pair(lambda q, cols: t[2, q, :, cols], 1, 0, 3, True)
-        gown[...] += times(wt, bx[g].reshape(512, 256))
-        goth[...] = times(w, bo[g].reshape(512, 256))
+    own_pair()
+    odd(chip_pair)
 
     c_f = copy(out3.at[0], in3.at[0], up1)
     c_g = copy(out3.at[1], in3.at[1], up2, "even")
@@ -298,23 +314,31 @@
     @even
     def _():
         arrive(early[2] + late[2])
-        pair(lambda q, cols: t[2, q, :, cols], 1, 3, 3, True)
-        out3[1] = times(wt, bx[g_up2].reshape(512, 256)).astype(BF)
+        weights(2, amplitudes(2), True)
+        out3[1] = times(wt[...], bx[g_up2]).astype(BF)
         c_g.start()
+
+    arrive(early[0] + late[0])
+    weights(0, amplitudes(0), True)
+    gf[...] = times(wt[...], bo[g_up1])
+    arrive(early[1] + late[1])
+    weights(1, amplitudes(1), True)
+    out3[0] = (gf[...] + times(wt[...], bx[g_up1])).astype(BF)
+    c_f.start()
+
+    @even
+    def _():
         cr_g.wait_recv()
-        goth[...] = times(w, rg[...].reshape(512, 256))
+        goth[...] = times(w[2], rg[...])
 
     cr_f.wait_recv()
-    arrive(early[0] + late[0])
-    pair(lambda q, cols: t[0, q, :, cols], 0, 2, 2, True)
-    gf[...] = times(wt, bo[g_up1].reshape(512, 256))
-    gown[...] += times(w, rf[...].reshape(512, 256))
-    arrive(early[1] + late[1])
-    pair(lambda q, cols: t[1, q, :, cols], 1, 2, 1, True)
-    out3[0] = (gf[...] + times(wt, bx[g_up1].reshape(512, 256))).astype(BF)
-    c_f.start()
-    out3[2] = (goth[...] + times(w, rf[...].reshape(512, 256))).astype(BF)
+    out3[2] = (goth[...] + times(w[1], rf[...])).astype(BF)
     c_x.start()
+    gown[...] += times(w[0], rf[...])
+    energy(3, own_amplitudes, 0, 0, 0)
+    energy(0, amplitudes(0), 0, 2, 2)
+    energy(1, amplitudes(1), 1, 2, 1)
+    energy(2, amplitudes(2), 1, 3 * (1 - k), 3)
 
     lane = lax.broadcasted_iota(jnp.int32, (8, 128), 1)
     total = [-jnp.sum(esum[n, 0:1], axis=1, keepdims=True) for n in range(4)]
@@ -372,8 +396,9 @@
             pltpu.VMEM((4, 128, 512), F32),
             pltpu.VMEM((512, 512), F32),
             pltpu.VMEM((512, 512), F32),
+            pltpu.VMEM((4, 512, 512), BF),
             pltpu.VMEM((512, 512), BF),
-            pltpu.VMEM((512, 512), BF),
+            pltpu.VMEM((4, 512, 512), BF),
             pltpu.VMEM((512, 256), F32),
             pltpu.VMEM((512, 256), F32),
             pltpu.VMEM((512, 256), F32),

time: 86.6 us -> 86.4 us (level)
  no operation moved by 1% of the time
where the time goes in v16:
time: 86.4 us; the launch traced here: 85.3 us
  Pallas kernels  81.1 us (94%)
  local copies, waits for them, and re-layouts  2.89 us (3%)
  between operations  1.29 us (1%)
    pallas_call x1, Pallas kernels, per_device(): pl.pallas_call(kernel, out_shape=(jax.ShapeDtypeStruct((256, 512), F32),...  81.1 us
    unnamed x4, local copies, waits for them, and re-layouts  2.89 us

profile of v16, /device:TPU:6, one launch (start us, length us, event | category | flops | bytes accessed | tf_op | source)
XLA Modules:
  0.0 85.3 jit_solution(14551930171100798517)
XLA Ops:
  1.3 81.1 %pairs.1 = (f32[256,512]{1,0:T(8,128)}, f32[1,4]{1,0:T(1,128)}) custom-call(bf16[256,512]{1,0:T(8,128)(2,1)} %bitcast.4, f32[1]{0:T(128)S(6)} %copy.7.occ_ref, f32[1,512]{1,0:T(1,128)} %bitcast.5), custom_call_target="tpu_custom_call" | custom-call | tf_op jit(solution)/shard_map/pairs/pallas_call | solution.py:378
  82.4 0.0 copy-start
  82.4 2.4 %copy.5 = f32[256,1,512]{2,1,0:T(1,128)} copy(f32[256,1,512]{2,0,1:T(8,128)} %bitcast.3) | data formatting | bytes 1048576
  84.7 0.0 copy-done
  84.8 0.5 copy.8
Async XLA Ops:
  82.4 2.4 %copy-start = (f32[1,4]{1,0:T(1,128)S(1)}, f32[1,4]{1,0:T(1,128)}, u32[]{:S(2)}) copy-start(f32[1,4]{1,0:T(1,128)} %get-tuple-element.10) | copy-start | bytes 52
